TPU v7x, 256 devices: a whole 4x4x8 slice. The times are simulated.
256 devices in a mesh: seq: 32 (over y, z), head: 8 (over x, core).
Axes of the slice: x: 4, y: 4, z: 8, core: 2. Of those that a mesh axis runs over, the one named last changes fastest.
Arguments:
- tokens: bfloat16 [16384, 2048], P('seq'), may hold values from -12 to 12
- w_qkv: bfloat16 [3, 2048, 2048], P(None, None, 'head'), may hold values from -1 to 1
- w_out: bfloat16 [2048, 2048], P('head'), may hold values from -1.5 to 1.5
- offsets: int32 [16], P('head'), may hold values from 0 to 7
- cotangent: bfloat16 [16384, 2048], P('seq'), may hold values from -6 to 6
Outputs:
- output: bfloat16 [16384, 2048], P('seq', 'head')
- input_grad: bfloat16 [16384, 2048], P('seq', 'head')
All inputs are finite; a program needn't handle non-finite values.
Results may differ from a plain program's by a relative error of at most 0.025.
Values may be sent and summed in bfloat16 or wider, within the bound.
A program may use at most 64 MiB of HBM per device.

v0:
```python
import math

import jax
import jax.numpy as jnp
from jax import lax
from jax.sharding import PartitionSpec as P

LEVELS = 4


def partner(value, axis, stride):
    mask = 2**stride
    pairs = [(source, source ^ mask) for source in range(lax.axis_size(axis))]
    return lax.ppermute(value, axis, pairs)


def selector(row_count, stride, phase):
    if stride == 1:
        return None
    picked = lax.broadcasted_iota(jnp.int32, (row_count // stride, row_count), 0)
    column = lax.broadcasted_iota(jnp.int32, (row_count // stride, row_count), 1)
    return column == picked * stride + phase


def pick_low(values, chooser):
    if chooser is None:
        return values
    return jnp.dot(chooser.astype(jnp.bfloat16), values, preferred_element_type=jnp.float32).astype(
        jnp.bfloat16
    )


def pick_stat(values, chooser):
    if chooser is None:
        return values
    return jnp.dot(
        chooser.astype(jnp.float32),
        values,
        precision=lax.Precision.HIGHEST,
        preferred_element_type=jnp.float32,
    )


def spread_wide(values, chooser):
    if chooser is None:
        return values
    return lax.dot_general(
        chooser.astype(jnp.float32),
        values,
        (((0,), (0,)), ((), ())),
        precision=lax.Precision.HIGHEST,
        preferred_element_type=jnp.float32,
    )


def spread_stat(values, chooser, fill):
    if chooser is None:
        return values
    wide = spread_wide(values[:, None], chooser)[:, 0]
    covered = jnp.any(chooser, axis=0)
    return jnp.where(covered, wide, fill)


def contract_last(left, right):
    return lax.dot_general(
        left, right, (((1,), (1,)), ((), ())), preferred_element_type=jnp.float32
    )


def contract_first(left, right):
    return lax.dot_general(
        left, right, (((0,), (0,)), ((), ())), preferred_element_type=jnp.float32
    )


def upper_half(seq_index, bit_pos):
    return seq_index // 2**bit_pos % 2 == 1


def joined_rows(own_part, far_part, upper_side):
    return jnp.where(
        upper_side,
        jnp.concatenate([far_part, own_part], 0),
        jnp.concatenate([own_part, far_part], 0),
    )


def grow(portion, level_k, seq_index):
    for bit_pos in range(level_k):
        far_part = partner(portion, "seq", bit_pos)
        portion = joined_rows(portion, far_part, upper_half(seq_index, bit_pos))
    return portion


def shrink(gradients, level_k, seq_index):
    for bit_pos in reversed(range(level_k)):
        half_rows = gradients.shape[0] // 2
        upper_side = upper_half(seq_index, bit_pos)
        sending = jnp.where(upper_side, gradients[:half_rows], gradients[half_rows:])
        keeping = jnp.where(upper_side, gradients[half_rows:], gradients[:half_rows])
        gradients = keeping + partner(sending.astype(jnp.bfloat16), "seq", bit_pos).astype(
            sending.dtype
        )
    return gradients


def on_device(tokens, w_qkv, w_out, offsets, cotangent):
    row_count = tokens.shape[0]
    head_count = offsets.shape[0]
    head_width = w_out.shape[0] // head_count
    scaling = 1.0 / math.sqrt(head_width)
    seq_index = lax.axis_index("seq")
    queries = (jnp.dot(tokens, w_qkv[0], preferred_element_type=jnp.float32) * scaling).astype(
        jnp.bfloat16
    )
    keys_all = jnp.dot(tokens, w_qkv[1], preferred_element_type=jnp.float32).astype(jnp.bfloat16)
    values_all = jnp.dot(tokens, w_qkv[2], preferred_element_type=jnp.float32).astype(jnp.bfloat16)
    choosers = [
        [
            selector(row_count, 2**level_k, offsets[head_pos] % 2**level_k)
            for level_k in range(LEVELS)
        ]
        for head_pos in range(head_count)
    ]
    pair_own = []
    for level_k in range(LEVELS):
        pieces = []
        for head_pos in range(head_count):
            first = head_pos * head_width
            pair = jnp.concatenate(
                [
                    keys_all[:, first : first + head_width],
                    values_all[:, first : first + head_width],
                ],
                1,
            )
            pieces.append(pick_low(pair, choosers[head_pos][level_k]))
        pair_own.append(jnp.concatenate(pieces, 1))
    pair_group = [grow(pair_own[level_k], level_k, seq_index) for level_k in range(LEVELS)]
    saved = []
    attended_heads = []
    for head_pos in range(head_count):
        first = head_pos * head_width
        query_head = queries[:, first : first + head_width]
        row_top = jnp.full((row_count,), -jnp.inf, jnp.float32)
        level_items = []
        for level_k in range(LEVELS):
            chooser = choosers[head_pos][level_k]
            query_sel = pick_low(query_head, chooser)
            key_sel = pair_group[level_k][:, 2 * first : 2 * first + head_width]
            value_sel = pair_group[level_k][:, 2 * first + head_width : 2 * first + 2 * head_width]
            logits = contract_last(query_sel, key_sel)
            row_top = jnp.maximum(
                row_top, spread_stat(jnp.max(logits, axis=1), chooser, jnp.float32(-jnp.inf))
            )
            level_items.append([query_sel, key_sel, value_sel, logits])
        totals = jnp.zeros((row_count,), jnp.float32)
        for level_k in range(LEVELS):
            chooser = choosers[head_pos][level_k]
            expo = jnp.exp(level_items[level_k][3] - pick_stat(row_top, chooser)[:, None])
            level_items[level_k][3] = expo
            totals = totals + spread_stat(jnp.sum(expo, axis=1), chooser, jnp.float32(0.0))
        attended_head = jnp.zeros((row_count, head_width), jnp.float32)
        for level_k in range(LEVELS):
            chooser = choosers[head_pos][level_k]
            weights = level_items[level_k][3] / pick_stat(totals, chooser)[:, None]
            weight_low = weights.astype(jnp.bfloat16)
            level_items[level_k][3] = weights
            level_items[level_k].append(weight_low)
            attended_sel = jnp.dot(
                weight_low, level_items[level_k][2], preferred_element_type=jnp.float32
            )
            attended_head = attended_head + spread_wide(attended_sel, chooser)
        attended_heads.append(attended_head.astype(jnp.bfloat16))
        saved.append(level_items)
    attended = jnp.concatenate(attended_heads, 1)
    partial_out = jnp.dot(attended, w_out, preferred_element_type=jnp.float32)
    output = lax.psum_scatter(
        partial_out.astype(jnp.bfloat16), "head", scatter_dimension=1, tiled=True
    )
    upstream = contract_last(cotangent, w_out).astype(jnp.bfloat16)
    grad_query_heads = []
    grad_pieces = [[] for level_k in range(LEVELS)]
    for head_pos in range(head_count):
        first = head_pos * head_width
        upstream_head = upstream[:, first : first + head_width]
        delta_head = jnp.sum(
            upstream_head.astype(jnp.float32) * attended_heads[head_pos].astype(jnp.float32), axis=1
        )
        grad_query = jnp.zeros((row_count, head_width), jnp.float32)
        for level_k in range(LEVELS):
            chooser = choosers[head_pos][level_k]
            query_sel, key_sel, value_sel, weights, weight_low = saved[head_pos][level_k]
            upstream_sel = pick_low(upstream_head, chooser)
            delta_sel = pick_stat(delta_head, chooser)
            inner = contract_last(upstream_sel, value_sel)
            slopes = (weights * (inner - delta_sel[:, None])).astype(jnp.bfloat16)
            grad_query = grad_query + spread_wide(
                jnp.dot(slopes, key_sel, preferred_element_type=jnp.float32), chooser
            )
            key_part = contract_first(slopes, query_sel)
            value_part = contract_first(weight_low, upstream_sel)
            grad_pieces[level_k].append(jnp.concatenate([key_part, value_part], 1))
        grad_query_heads.append((grad_query * scaling).astype(jnp.bfloat16))
    grad_parts = [jnp.concatenate(grad_pieces[level_k], 1) for level_k in range(LEVELS)]
    own_grads = [shrink(grad_parts[level_k], level_k, seq_index) for level_k in range(LEVELS)]
    grad_key_heads = []
    grad_value_heads = []
    for head_pos in range(head_count):
        first = head_pos * head_width
        grad_pair = jnp.zeros((row_count, 2 * head_width), jnp.float32)
        for level_k in range(LEVELS):
            grad_pair = grad_pair + spread_wide(
                own_grads[level_k][:, 2 * first : 2 * first + 2 * head_width],
                choosers[head_pos][level_k],
            )
        grad_key_heads.append(grad_pair[:, :head_width].astype(jnp.bfloat16))
        grad_value_heads.append(grad_pair[:, head_width:].astype(jnp.bfloat16))
    partial_in = contract_last(jnp.concatenate(grad_query_heads, 1), w_qkv[0])
    partial_in = partial_in + contract_last(jnp.concatenate(grad_key_heads, 1), w_qkv[1])
    partial_in = partial_in + contract_last(jnp.concatenate(grad_value_heads, 1), w_qkv[2])
    input_grad = lax.psum_scatter(
        partial_in.astype(jnp.bfloat16), "head", scatter_dimension=1, tiled=True
    )
    return (output, input_grad)


def solution(mesh):
    in_specs = (P("seq", None), P(None, None, "head"), P("head", None), P("head"), P("seq", None))
    out_specs = (P("seq", "head"), P("seq", "head"))
    return jax.shard_map(
        on_device, mesh=mesh, in_specs=in_specs, out_specs=out_specs, check_vma=False
    )
```

profile of v0, /device:TPU:1, one launch (start us, length us, event | category | flops | bytes accessed | tf_op | source)
XLA Modules:
  0.0 211.6 jit_solution(4171575571745083306)
XLA Ops:
  7.2 1.4 fusion.319
  12.5 2.7 %convolution_convert_fusion.2 = bf16[512,256]{0,1:T(8,128)(2,1)} fusion(bf16[512,2048]{1,0:T(8,128)(2,1)S(1)} %copy-done, bf16[3,2048,256]{2,1,0:T(8,128)(2,1)} %param.6), kind=kOutput, calls=%fused_computation.25 | convolution fusion | flops 537001984 | bytes 3407872 | tf_op jit(solution)/shard_map/dot_general | solution.py:117
  15.2 2.0 convolution_convert_fusion.3
  17.3 1.1 fusion.317
  19.9 2.6 %collective-permute-start.3 = (bf16[64,512]{1,0:T(8,128)(2,1)}, bf16[64,512]{1,0:T(8,128)(2,1)}, u32[]{:S(2)}, u32[]{:S(2)}) collective-permute-start(bf16[64,512]{1,0:T(8,128)(2,1)} %pad_maximum_fusion.13), channel_id=1, source_target_pairs={{0,8},{8,0},{16,24},{24,16},{32,40},{40,32},{48,56},{56,48},{64,72... | collective-permute-start | bytes 196616 | tf_op jit(solution)/shard_map/ppermute | solution.py:14
  22.4 1.2 convolution_convert_fusion.10
  23.6 1.2 convolution_convert_fusion.9
  25.6 1.3 convolution_convert_fusion.5
  26.9 1.3 convolution_convert_fusion.4
  29.0 1.4 collective-permute-start
  31.8 1.3 fusion.88
  33.7 2.3 %convolution_convert_fusion.1 = bf16[512,256]{0,1:T(8,128)(2,1)S(1)} fusion(bf16[512,2048]{1,0:T(8,128)(2,1)} %param.9, bf16[256,2048]{1,0:T(8,128)(2,1)S(1)} %copy-done.11), kind=kOutput, calls=%fused_computation.24 | convolution fusion | flops 537001984 | bytes 3407872 | tf_op jit(solution)/shard_map/dot_general | solution.py:65
  41.1 1.9 fusion.12
  48.5 1.9 fusion.326
  52.1 3.1 %collective-permute-start.4 = (bf16[128,512]{1,0:T(8,128)(2,1)S(1)}, bf16[128,512]{1,0:T(8,128)(2,1)}, u32[]{:S(2)}, u32[]{:S(2)}) collective-permute-start(bf16[128,512]{1,0:T(8,128)(2,1)S(1)} %maximum_select_fusion.5), channel_id=1, source_target_pairs={{0,16},{8,24},{16,0},{24,8},{32,48},{40,56},{48,32},{56,40},{64,80... | collective-permute-start | bytes 393224 | tf_op jit(solution)/shard_map/ppermute | solution.py:14
  55.2 1.3 fusion.142
  56.5 1.2 maximum_select_fusion.3
  57.8 3.6 %collective-permute-done.4 = bf16[128,512]{1,0:T(8,128)(2,1)} collective-permute-done((bf16[128,512]{1,0:T(8,128)(2,1)S(1)}, bf16[128,512]{1,0:T(8,128)(2,1)}, u32[]{:S(2)}, u32[]{:S(2)}) %collective-permute-start.4) | collective-permute-done | bytes 131104 | tf_op jit(solution)/shard_map/ppermute | solution.py:14
  61.4 1.0 maximum_select_fusion.4
  62.5 11.4 %collective-permute-start.5 = (bf16[256,512]{1,0:T(8,128)(2,1)S(1)}, bf16[256,512]{1,0:T(8,128)(2,1)S(1)}, u32[]{:S(2)}, u32[]{:S(2)}) collective-permute-start(bf16[256,512]{1,0:T(8,128)(2,1)S(1)} %maximum_select_fusion.4), channel_id=1, source_target_pairs={{0,32},{8,40},{16,48},{24,56},{32,0},{40,8},{48,16},{56,24},{64,96... | collective-permute-start | bytes 786440 | tf_op jit(solution)/shard_map/ppermute | solution.py:14
  73.8 1.4 maximum_select_fusion
  75.3 1.1 fusion.323
  76.4 1.1 fusion.327
  79.6 2.3 %collective-permute-done.5 = bf16[256,512]{1,0:T(8,128)(2,1)S(1)} collective-permute-done((bf16[256,512]{1,0:T(8,128)(2,1)S(1)}, bf16[256,512]{1,0:T(8,128)(2,1)S(1)}, u32[]{:S(2)}, u32[]{:S(2)}) %collective-permute-start.5) | collective-permute-done | bytes 262176 | tf_op jit(solution)/shard_map/ppermute | solution.py:14
  92.2 1.0 fusion.251
  102.8 1.1 fusion.129
  105.4 1.1 fusion.125
  110.3 1.2 fusion.216
  111.5 1.0 fusion.298
  112.6 1.2 fusion.138
  113.7 1.2 fusion.133
  117.6 1.0 fusion.295
  118.6 5.2 %collective-permute-start.7 = (bf16[256,512]{1,0:T(8,128)(2,1)}, bf16[256,512]{1,0:T(8,128)(2,1)}, u32[]{:S(2)}, u32[]{:S(2)}) collective-permute-start(bf16[256,512]{1,0:T(8,128)(2,1)} %select_convert_fusion.1), channel_id=1, source_target_pairs={{0,16},{8,24},{16,0},{24,8},{32,48},{40,56},{48,32},{56,40},{64,80... | collective-permute-start | bytes 786440 | tf_op jit(solution)/shard_map/ppermute | solution.py:14
  123.8 3.6 %collective-permute-start.9 = (bf16[256,512]{0,1:T(8,128)(2,1)}, bf16[256,512]{0,1:T(8,128)(2,1)}, u32[]{:S(2)}, u32[]{:S(2)}) collective-permute-start(bf16[256,512]{0,1:T(8,128)(2,1)} %select_convert_fusion), channel_id=1, source_target_pairs={{0,32},{8,40},{16,48},{24,56},{32,0},{40,8},{48,16},{56,24},{64,96... | collective-permute-start | bytes 786440 | tf_op jit(solution)/shard_map/ppermute | solution.py:14
  127.4 2.1 convolution_convert_fusion
  130.3 1.7 convolution_add_fusion.5
  132.0 1.5 fusion.26
  133.5 1.5 fusion.28
  135.1 2.0 fusion.38
  137.3 2.0 collective-permute-start.6
  139.6 6.6 %collective-permute-done.7 = bf16[256,512]{1,0:T(8,128)(2,1)} collective-permute-done((bf16[256,512]{1,0:T(8,128)(2,1)}, bf16[256,512]{1,0:T(8,128)(2,1)}, u32[]{:S(2)}, u32[]{:S(2)}) %collective-permute-start.7) | collective-permute-done | bytes 262176 | tf_op jit(solution)/shard_map/ppermute | solution.py:14
  146.2 1.1 convert_add_fusion.1
  147.5 1.0 convert_add_fusion
  148.5 1.5 collective-permute-start.10
  150.1 4.6 %collective-permute-done.6 = bf16[256,512]{1,0:T(8,128)(2,1)S(1)} collective-permute-done((bf16[256,512]{1,0:T(8,128)(2,1)S(1)}, bf16[256,512]{1,0:T(8,128)(2,1)S(1)}, u32[]{:S(2)}, u32[]{:S(2)}) %collective-permute-start.6) | collective-permute-done | bytes 262176 | tf_op jit(solution)/shard_map/ppermute | solution.py:14
  155.9 3.0 %collective-permute-done.8 = bf16[128,512]{1,0:T(8,128)(2,1)S(1)} collective-permute-done((bf16[128,512]{1,0:T(8,128)(2,1)S(1)}, bf16[128,512]{1,0:T(8,128)(2,1)S(1)}, u32[]{:S(2)}, u32[]{:S(2)}) %collective-permute-start.8) | collective-permute-done | bytes 131104 | tf_op jit(solution)/shard_map/ppermute | solution.py:14
  163.4 2.1 add_convert_fusion
  165.5 39.2 %reduce-scatter.5.cloned.1.call-done = bf16[512,256]{1,0:T(8,128)(2,1)} async-done(((bf16[512,2048]{1,0:T(8,128)(2,1)}), bf16[512,256]{1,0:T(8,128)(2,1)}) %reduce-scatter.5.cloned.1.call-update) | async-done | bytes 262160 | tf_op jit(solution)/shard_map/reduce_scatter | solution.py:222
  (306 shorter events, 53.7 us)
Async XLA Ops:
  7.2 158.4 %reduce-scatter.3.cloned.1.call-start = ((), (), s32[]{:S(2)}) async-start(), calls=%async_computation.2 | async-start | bytes 2359296 | tf_op jit(solution)/shard_map/reduce_scatter | solution.py:178
  17.2 16.5 %copy-start.11 = (bf16[256,2048]{1,0:T(8,128)(2,1)S(1)}, bf16[256,2048]{1,0:T(8,128)(2,1)}, u32[]{:S(2)}) copy-start(bf16[256,2048]{1,0:T(8,128)(2,1)} %param.7) | copy-start | bytes 3145732
  17.2 25.8 %copy-start.51 = (s32[64]{0:T(128)}, s32[64]{0:T(128)S(1)}, u32[]{:S(2)}) copy-start(s32[64]{0:T(128)S(1)} %fusion.276) | copy-start | bytes 772
  17.3 8.3 %copy-start.54 = (s32[64]{0:T(128)}, s32[64]{0:T(128)S(1)}, u32[]{:S(2)}) copy-start(s32[64]{0:T(128)S(1)} %fusion.275) | copy-start | bytes 772
  19.9 31.2 %collective-permute-start.3 = (bf16[64,512]{1,0:T(8,128)(2,1)}, bf16[64,512]{1,0:T(8,128)(2,1)}, u32[]{:S(2)}, u32[]{:S(2)}) collective-permute-start(bf16[64,512]{1,0:T(8,128)(2,1)} %pad_maximum_fusion.13), channel_id=1, source_target_pairs={{0,8},{8,0},{16,24},{24,16},{32,40},{40,32},{48,56},{56,48},{64,72... | collective-permute-start | bytes 196616 | tf_op jit(solution)/shard_map/ppermute | solution.py:14
  22.4 15.2 %copy-start.47 = (s32[128]{0:T(128)}, s32[128]{0:T(128)S(1)}, u32[]{:S(2)}) copy-start(s32[128]{0:T(128)S(1)} %fusion.278) | copy-start | bytes 1540
  25.5 31.0 %collective-permute-start.1 = (bf16[128,512]{1,0:T(8,128)(2,1)}, bf16[128,512]{1,0:T(8,128)(2,1)}, u32[]{:S(2)}, u32[]{:S(2)}) collective-permute-start(bf16[128,512]{1,0:T(8,128)(2,1)} %pad_maximum_fusion.6), channel_id=1, source_target_pairs={{0,8},{8,0},{16,24},{24,16},{32,40},{40,32},{48,56},{56,48},{64,72... | collective-permute-start | bytes 393224 | tf_op jit(solution)/shard_map/ppermute | solution.py:14
  25.6 13.7 %copy-start.37 = (s32[256]{0:T(256)}, s32[256]{0:T(256)S(1)}, u32[]{:S(2)}) copy-start(s32[256]{0:T(256)S(1)} %fusion.270) | copy-start | bytes 3076
  25.6 14.6 %copy-start.41 = (s32[256]{0:T(256)}, s32[256]{0:T(256)S(1)}, u32[]{:S(2)}) copy-start(s32[256]{0:T(256)S(1)} %fusion.269) | copy-start | bytes 3076
  28.3 8.5 %copy-start.55 = (s32[64]{0:T(128)S(1)}, s32[64]{0:T(128)}, u32[]{:S(2)}) copy-start(s32[64]{0:T(128)} %copy-done.54) | copy-start | bytes 772
  29.0 44.8 %collective-permute-start = (bf16[256,512]{0,1:T(8,128)(2,1)}, bf16[256,512]{0,1:T(8,128)(2,1)}, u32[]{:S(2)}, u32[]{:S(2)}) collective-permute-start(bf16[256,512]{0,1:T(8,128)(2,1)} %pad_maximum_fusion.5), channel_id=1, source_target_pairs={{0,8},{8,0},{16,24},{24,16},{32,40},{40,32},{48,56},{56,48},{64,72... | collective-permute-start | bytes 786440 | tf_op jit(solution)/shard_map/ppermute | solution.py:14
  30.4 8.1 %copy-start.59 = (s32[128]{0:T(128)S(1)}, s32[128]{0:T(128)}, u32[]{:S(2)}) copy-start(s32[128]{0:T(128)} %copy-done.58) | copy-start | bytes 1540
  52.1 9.3 %collective-permute-start.4 = (bf16[128,512]{1,0:T(8,128)(2,1)S(1)}, bf16[128,512]{1,0:T(8,128)(2,1)}, u32[]{:S(2)}, u32[]{:S(2)}) collective-permute-start(bf16[128,512]{1,0:T(8,128)(2,1)S(1)} %maximum_select_fusion.5), channel_id=1, source_target_pairs={{0,16},{8,24},{16,0},{24,8},{32,48},{40,56},{48,32},{56,40},{64,80... | collective-permute-start | bytes 393224 | tf_op jit(solution)/shard_map/ppermute | solution.py:14
  56.5 21.1 %copy-start.43 = (s32[256]{0:T(256)S(1)}, s32[256]{0:T(256)}, u32[]{:S(2)}) copy-start(s32[256]{0:T(256)} %copy-done.41) | copy-start | bytes 3076
  56.5 21.4 %copy-start.39 = (s32[256]{0:T(256)S(1)}, s32[256]{0:T(256)}, u32[]{:S(2)}) copy-start(s32[256]{0:T(256)} %copy-done.37) | copy-start | bytes 3076
  56.5 22.0 %copy-start.34 = (bf16[128,128]{1,0:T(8,128)(2,1)S(1)}, bf16[128,128]{1,0:T(8,128)(2,1)}, u32[]{:S(2)}) copy-start(bf16[128,128]{1,0:T(8,128)(2,1)} %convolution_convert_fusion.14) | copy-start | bytes 98308
  56.5 22.2 %copy-start.35 = (bf16[128,128]{1,0:T(8,128)(2,1)S(1)}, bf16[128,128]{1,0:T(8,128)(2,1)}, u32[]{:S(2)}) copy-start(bf16[128,128]{1,0:T(8,128)(2,1)} %convolution_convert_fusion.17) | copy-start | bytes 98308
  56.5 22.5 %copy-start.60 = (s32[128]{0:T(128)S(1)}, s32[128]{0:T(128)}, u32[]{:S(2)}) copy-start(s32[128]{0:T(128)} %copy-done.58) | copy-start | bytes 1540
  56.5 22.8 %copy-start.49 = (s32[128]{0:T(128)S(1)}, s32[128]{0:T(128)}, u32[]{:S(2)}) copy-start(s32[128]{0:T(128)} %copy-done.47) | copy-start | bytes 1540
  57.7 20.5 %collective-permute-start.2 = (bf16[256,512]{1,0:T(8,128)(2,1)S(1)}, bf16[256,512]{1,0:T(8,128)(2,1)S(1)}, u32[]{:S(2)}, u32[]{:S(2)}) collective-permute-start(bf16[256,512]{1,0:T(8,128)(2,1)S(1)} %maximum_select_fusion.3), channel_id=1, source_target_pairs={{0,16},{8,24},{16,0},{24,8},{32,48},{40,56},{48,32},{56,40},{64,80... | collective-permute-start | bytes 786440 | tf_op jit(solution)/shard_map/ppermute | solution.py:14
  62.4 19.9 %copy-start.56 = (s32[64]{0:T(128)S(1)}, s32[64]{0:T(128)}, u32[]{:S(2)}) copy-start(s32[64]{0:T(128)} %copy-done.54) | copy-start | bytes 772
  62.4 20.2 %copy-start.46 = (f32[512]{0:T(512)S(1)}, f32[512]{0:T(512)}, u32[]{:S(2)}) copy-start(f32[512]{0:T(512)} %get-tuple-element.18) | copy-start | bytes 6148
  62.4 20.2 %copy-start.64 = (pred[512]{0:T(512)(128)(4,1)S(1)}, pred[512]{0:T(512)(128)(4,1)}, u32[]{:S(2)}) copy-start(pred[512]{0:T(512)(128)(4,1)} %fusion.57) | copy-start | bytes 1540
  62.4 20.2 %copy-start.65 = (pred[512]{0:T(512)(128)(4,1)S(1)}, pred[512]{0:T(512)(128)(4,1)}, u32[]{:S(2)}) copy-start(pred[512]{0:T(512)(128)(4,1)} %fusion.88) | copy-start | bytes 1540
  62.5 20.2 %copy-start.67 = (pred[512]{0:T(512)(128)(4,1)S(1)}, pred[512]{0:T(512)(128)(4,1)}, u32[]{:S(2)}) copy-start(pred[512]{0:T(512)(128)(4,1)} %fusion.137) | copy-start | bytes 1540
  62.5 19.4 %collective-permute-start.5 = (bf16[256,512]{1,0:T(8,128)(2,1)S(1)}, bf16[256,512]{1,0:T(8,128)(2,1)S(1)}, u32[]{:S(2)}, u32[]{:S(2)}) collective-permute-start(bf16[256,512]{1,0:T(8,128)(2,1)S(1)} %maximum_select_fusion.4), channel_id=1, source_target_pairs={{0,32},{8,40},{16,48},{24,56},{32,0},{40,8},{48,16},{56,24},{64,96... | collective-permute-start | bytes 786440 | tf_op jit(solution)/shard_map/ppermute | solution.py:14
  78.7 7.7 %copy-start.36 = (bf16[64,128]{1,0:T(8,128)(2,1)S(1)}, bf16[64,128]{1,0:T(8,128)(2,1)}, u32[]{:S(2)}) copy-start(bf16[64,128]{1,0:T(8,128)(2,1)} %convolution_convert_fusion.21) | copy-start | bytes 49156
  79.0 7.7 %copy-start.52 = (s32[64]{0:T(128)S(1)}, s32[64]{0:T(128)}, u32[]{:S(2)}) copy-start(s32[64]{0:T(128)} %copy-done.51) | copy-start | bytes 772
  79.3 7.6 %copy-start.45 = (f32[512]{0:T(512)S(1)}, f32[512]{0:T(512)}, u32[]{:S(2)}) copy-start(f32[512]{0:T(512)} %get-tuple-element.26) | copy-start | bytes 6148
  79.3 7.6 %copy-start.62 = (pred[512]{0:T(512)(128)(4,1)S(1)}, pred[512]{0:T(512)(128)(4,1)}, u32[]{:S(2)}) copy-start(pred[512]{0:T(512)(128)(4,1)} %fusion.64) | copy-start | bytes 1540
  79.3 7.6 %copy-start.63 = (pred[512]{0:T(512)(128)(4,1)S(1)}, pred[512]{0:T(512)(128)(4,1)}, u32[]{:S(2)}) copy-start(pred[512]{0:T(512)(128)(4,1)} %fusion.92) | copy-start | bytes 1540
  79.3 7.6 %copy-start.66 = (pred[512]{0:T(512)(128)(4,1)S(1)}, pred[512]{0:T(512)(128)(4,1)}, u32[]{:S(2)}) copy-start(pred[512]{0:T(512)(128)(4,1)} %fusion.142) | copy-start | bytes 1540
  82.6 6.7 %copy-start.1 = (f32[512,512]{0,1:T(8,128)S(1)}, f32[512,512]{0,1:T(8,128)}, u32[]{:S(2)}) copy-start(f32[512,512]{0,1:T(8,128)} %get-tuple-element.27) | copy-start | bytes 3145732
  98.8 18.8 %copy-start.5 = (bf16[512,512]{0,1:T(8,128)(2,1)}, bf16[512,512]{0,1:T(8,128)(2,1)S(1)}, u32[]{:S(2)}) copy-start(bf16[512,512]{0,1:T(8,128)(2,1)S(1)} %fusion.2) | copy-start | bytes 1572868
  114.9 12.5 %copy-start.12 = (bf16[256,2048]{1,0:T(8,128)(2,1)S(1)}, bf16[256,2048]{1,0:T(8,128)(2,1)}, u32[]{:S(2)}) copy-start(bf16[256,2048]{1,0:T(8,128)(2,1)} %param.7) | copy-start | bytes 3145732
  117.6 12.0 %copy-start.40 = (s32[256]{0:T(256)S(1)}, s32[256]{0:T(256)}, u32[]{:S(2)}) copy-start(s32[256]{0:T(256)} %copy-done.37) | copy-start | bytes 3076
  118.6 10.9 %copy-start.10 = (f32[512,128]{1,0:T(8,128)S(1)}, f32[512,128]{1,0:T(8,128)}, u32[]{:S(2)}) copy-start(f32[512,128]{1,0:T(8,128)} %fusion.298) | copy-start | bytes 786436
  118.6 11.7 %copy-start.44 = (s32[256]{0:T(256)S(1)}, s32[256]{0:T(256)}, u32[]{:S(2)}) copy-start(s32[256]{0:T(256)} %copy-done.41) | copy-start | bytes 3076
  118.6 27.6 %collective-permute-start.7 = (bf16[256,512]{1,0:T(8,128)(2,1)}, bf16[256,512]{1,0:T(8,128)(2,1)}, u32[]{:S(2)}, u32[]{:S(2)}) collective-permute-start(bf16[256,512]{1,0:T(8,128)(2,1)} %select_convert_fusion.1), channel_id=1, source_target_pairs={{0,16},{8,24},{16,0},{24,8},{32,48},{40,56},{48,32},{56,40},{64,80... | collective-permute-start | bytes 786440 | tf_op jit(solution)/shard_map/ppermute | solution.py:14
  123.8 23.7 %collective-permute-start.9 = (bf16[256,512]{0,1:T(8,128)(2,1)}, bf16[256,512]{0,1:T(8,128)(2,1)}, u32[]{:S(2)}, u32[]{:S(2)}) collective-permute-start(bf16[256,512]{0,1:T(8,128)(2,1)} %select_convert_fusion), channel_id=1, source_target_pairs={{0,32},{8,40},{16,48},{24,56},{32,0},{40,8},{48,16},{56,24},{64,96... | collective-permute-start | bytes 786440 | tf_op jit(solution)/shard_map/ppermute | solution.py:14
  129.5 75.2 %reduce-scatter.5.cloned.1.call-start = ((), (), s32[]{:S(2)}) async-start(), calls=%async_computation.3 | async-start | bytes 2359296 | tf_op jit(solution)/shard_map/reduce_scatter | solution.py:222
  137.2 9.1 %copy-start.3 = (f32[512,512]{1,0:T(8,128)S(1)}, f32[512,512]{1,0:T(8,128)}, u32[]{:S(2)}) copy-start(f32[512,512]{1,0:T(8,128)} %copy-done.2) | copy-start | bytes 3145732
  137.3 17.3 %collective-permute-start.6 = (bf16[256,512]{1,0:T(8,128)(2,1)S(1)}, bf16[256,512]{1,0:T(8,128)(2,1)S(1)}, u32[]{:S(2)}, u32[]{:S(2)}) collective-permute-start(bf16[256,512]{1,0:T(8,128)(2,1)S(1)} %select_convert_fusion.2), channel_id=1, source_target_pairs={{0,8},{8,0},{16,24},{24,16},{32,40},{40,32},{48,56},{56,48},{64,72... | collective-permute-start | bytes 786440 | tf_op jit(solution)/shard_map/ppermute | solution.py:14
  147.3 11.5 %collective-permute-start.8 = (bf16[128,512]{1,0:T(8,128)(2,1)S(1)}, bf16[128,512]{1,0:T(8,128)(2,1)S(1)}, u32[]{:S(2)}, u32[]{:S(2)}) collective-permute-start(bf16[128,512]{1,0:T(8,128)(2,1)S(1)} %select_convert_fusion.5), channel_id=1, source_target_pairs={{0,8},{8,0},{16,24},{24,16},{32,40},{40,32},{48,56},{56,48},{64,72... | collective-permute-start | bytes 393224 | tf_op jit(solution)/shard_map/ppermute | solution.py:14
  148.5 12.1 %copy-start.57 = (s32[64]{0:T(128)S(1)}, s32[64]{0:T(128)}, u32[]{:S(2)}) copy-start(s32[64]{0:T(128)} %copy-done.54) | copy-start | bytes 772
  148.5 12.5 %copy-start.15 = (f32[512,128]{0,1:T(8,128)S(1)}, f32[512,128]{0,1:T(8,128)}, u32[]{:S(2)}) copy-start(f32[512,128]{0,1:T(8,128)} %fusion.251) | copy-start | bytes 786436
  148.5 6.3 %collective-permute-start.10 = (bf16[128,512]{0,1:T(8,128)(2,1)S(1)}, bf16[128,512]{0,1:T(8,128)(2,1)S(1)}, u32[]{:S(2)}, u32[]{:S(2)}) collective-permute-start(bf16[128,512]{0,1:T(8,128)(2,1)S(1)} %select_convert_fusion.4), channel_id=1, source_target_pairs={{0,16},{8,24},{16,0},{24,8},{32,48},{40,56},{48,32},{56,40},{64,80... | collective-permute-start | bytes 393224 | tf_op jit(solution)/shard_map/ppermute | solution.py:14
  155.0 5.5 %collective-permute-start.11 = (bf16[64,512]{0,1:T(8,128)(2,1)S(1)}, bf16[64,512]{0,1:T(8,128)(2,1)S(1)}, u32[]{:S(2)}, u32[]{:S(2)}) collective-permute-start(bf16[64,512]{0,1:T(8,128)(2,1)S(1)} %select_convert_fusion.3), channel_id=1, source_target_pairs={{0,8},{8,0},{16,24},{24,16},{32,40},{40,32},{48,56},{56,48},{64,72... | collective-permute-start | bytes 196616 | tf_op jit(solution)/shard_map/ppermute | solution.py:14
  (40 other events, 123.3 us)
Sparse Core Ops, SparseCore 0:
  129.6 33.6 reduce-scatter.2
  166.4 38.2 reduce-scatter.4
where the time goes:
time: 214 us; the launch traced here: 212 us
  matrix products  77.5 us (36%)
  waiting for transfers between devices  59.9 us (28%)
  starting transfers between devices  31.9 us (15%)
  between operations  19.3 us (9%)
  other arithmetic  18.7 us (9%)
  local copies, waits for them, and re-layouts  4.22 us (2%)
    reduce_scatter x1, waiting for transfers between devices, on_device(): lax.psum_scatter(partial_in.astype(jnp.bfloat16), 'head', scatter_dimensi...  39.2 us
    ppermute x12, starting transfers between devices, partner(): return lax.ppermute(value, axis, pairs)  31.9 us
    ppermute x12, waiting for transfers between devices, partner(): return lax.ppermute(value, axis, pairs)  20.7 us
    dot_general x30, matrix products, spread_wide(): lax.dot_general(chooser.astype(jnp.float32), values, (((0,), (0,)), ((),...  16.1 us
    dot_general x20, matrix products, contract_last(): lax.dot_general(left, right, (((1,), (1,)), ((), ())), preferred_element_...  15.4 us
    dot_general x18, matrix products, pick_low(): jnp.dot(chooser.astype(jnp.bfloat16), values, preferred_element_type=jnp....  15 us
    dot_general x16, matrix products, contract_first(): lax.dot_general(left, right, (((0,), (0,)), ((), ())), preferred_element_...  9.69 us
    dot_general x18, matrix products, pick_stat(): jnp.dot(chooser.astype(jnp.float32), values, precision=lax.Precision.HIGH...  5.59 us
  transfers between devices with their start and end apart: 14, of which 7 were waited for; matrix products, arithmetic and copies ran while one was open for 26% of the time, Pallas kernels for 0%

commit v1 on v0

v1 whole, which is shorter than its diff:
```python
import math

import jax
import jax.numpy as jnp
from jax import lax
from jax.experimental import pallas as pl
from jax.experimental.pallas import tpu as pltpu
from jax.sharding import PartitionSpec as P

MESH = pl.DeviceIdType.MESH
F32, BF16 = jnp.float32, jnp.bfloat16
ROWS = 512
MODEL = 2048
HD = 128
HEADS = 2
RING = 8
ALL = 1280
PAIR, QUAD0, QUAD1, OCT0, OCT1, OCT2, OCT3 = 512, 768, 896, 1024, 1088, 1152, 1216
COLS = 256
NEG = float("-inf")


def nn(a, b):
    return jnp.dot(a, b, preferred_element_type=F32)


def nt(a, b):
    return lax.dot_general(a, b, (((1,), (1,)), ((), ())), preferred_element_type=F32)


def tn(a, b):
    return lax.dot_general(a, b, (((0,), (0,)), ((), ())), preferred_element_type=F32)


def slot_table():
    tables = []
    for k in range(1, RING):
        code = 0
        for d in range(RING):
            source = (d - k) % RING
            inner = d % 4 in (1, 2)
            side = 1 if d % 2 == 1 else -1
            out_dist = (source - d) * side % RING
            in_dist = (d - source) * side % RING
            if source // 2 == d // 2:
                slot = 0
            elif source // 4 == d // 4:
                slot = 1 if source % 4 in (1, 2) else 2
            elif inner:
                slot = {2: 3, 3: 4}[in_dist] if in_dist in (2, 3) else {3: 5, 4: 6}[out_dist]
            else:
                slot = 2 + out_dist
            code += slot * 8**d
        tables.append(code)
    return tables


SLOTS = slot_table()


def kernel(
    tok_hbm, wqkv_hbm, wo_hbm, off_ref, cot_hbm, out_ref, ing_ref,
    tok, wqkv, wo, cot, raw, kv, qd, perm, unperm, mask_a, mask_b, mask_p, mask_q,
    grads, att_p, gcat, att, gall, stat, stat_g,
    own, sib_out, sib_in, far, half_in, near, near_in,
    load_sem, kv_send, kv_recv, qd_send, qd_recv, st_send, st_recv, rs_send, rs_recv,
):
    seq = lax.axis_index("seq")
    head = lax.axis_index("head")
    z = lax.rem(seq, RING)
    base = seq - z
    odd = lax.rem(z, 2)
    partner = (base + z + 1 - 2 * odd, head)
    outer = (base + lax.rem(z + 2 * odd + RING - 1, RING), head)
    inner = lax.rem((lax.rem(z, 4) + 1) // 2, 2) == 1
    edge = jnp.logical_not(inner)
    x, core = head // 2, lax.rem(head, 2)
    sibling = (seq, head + 1 - 2 * core)
    right = (seq, lax.rem(x + 1, 4) * 2 + core)
    left = (seq, lax.rem(x + 3, 4) * 2 + core)

    loads = [
        pltpu.make_async_copy(tok_hbm, tok, load_sem.at[0]),
        pltpu.make_async_copy(wqkv_hbm.at[1], wqkv.at[1], load_sem.at[1]),
        pltpu.make_async_copy(wqkv_hbm.at[2], wqkv.at[2], load_sem.at[2]),
        pltpu.make_async_copy(wqkv_hbm.at[0], wqkv.at[0], load_sem.at[3]),
        pltpu.make_async_copy(cot_hbm, cot, load_sem.at[4]),
        pltpu.make_async_copy(wo_hbm, wo, load_sem.at[5]),
    ]
    for copy in loads:
        copy.start()

    barrier = pltpu.get_barrier_semaphore()
    peers = [(base + lax.rem(z + k, RING), head) for k in range(1, RING)]
    for device in peers + [sibling, right, left]:
        pl.semaphore_signal(barrier, inc=1, device_id=device, device_id_type=MESH)

    index = lax.broadcasted_iota(jnp.int32, (ROWS, 128), 0)
    lane = lax.broadcasted_iota(jnp.int32, (ROWS, 128), 1)
    for h in range(HEADS):
        offset = off_ref[h]
        block = index >> 6
        turned = ((block & 1) << 2) | (block & 2) | (block >> 2)
        old = ((index & 63) << 3) + ((turned + offset) & 7)
        rest = ((index & 7) - offset) & 7
        new = ((((rest & 1) << 2) | (rest & 2) | (rest >> 2)) << 6) + (index >> 3)
        for c in range(ROWS // 128):
            perm[h, :, c * 128 : (c + 1) * 128] = jnp.where(old == lane + c * 128, 1.0, 0.0).astype(BF16)
            unperm[h, :, c * 128 : (c + 1) * 128] = jnp.where(new == lane + c * 128, 1.0, 0.0).astype(BF16)

    def levels(key, query, start):
        far_end = jnp.maximum(key, query)
        count = jnp.full(key.shape, float(start), F32)
        for limit in (256, 128, 64):
            count = count + jnp.where(far_end < limit, 1.0, 0.0)
        return count

    mask_a[0:512] = levels(index, lane, 1)
    mask_a[512:768] = levels(index[0:256], lane[0:256], 0)
    quad_mask = levels(index[0:128], lane[0:128], -1)
    mask_a[768:896] = quad_mask
    mask_a[896:1024] = quad_mask
    mask_a[1024:1280] = jnp.where(lane[0:256] < 64, 1.0, 0.0)
    mask_b[0:512] = levels(index, lane + 128, 1)
    mask_b[512:768] = levels(index[0:256], lane[0:256] + 128, 0)
    mask_p[:, 0:128] = levels(index[0:256], lane[0:256], 0)
    mask_p[:, 128:256] = levels(index[0:256], lane[0:256] + 128, 0)
    mask_q[:, 0:128] = quad_mask
    mask_q[:, 128:256] = quad_mask

    def project(left_part, right_part):
        for h in range(HEADS):
            raw[:, h * 256 : h * 256 + 128] = left_part[:, h * 128 : (h + 1) * 128]
            raw[:, h * 256 + 128 : h * 256 + 256] = right_part[:, h * 128 : (h + 1) * 128]

    def permute(into):
        for h in range(HEADS):
            into[0:ROWS, h * 256 : (h + 1) * 256] = nn(perm[h], raw[:, h * 256 : (h + 1) * 256]).astype(BF16)

    def remote(src, dst, send, recv, device):
        return pltpu.make_async_remote_copy(
            src_ref=src, dst_ref=dst, send_sem=send, recv_sem=recv, device_id=device, device_id_type=MESH
        )

    steps = {
        "p1": ((0, 256, PAIR), (0, 256, PAIR), partner),
        "o1": ((0, 128, QUAD0), (0, 64, OCT0), outer),
        "o2": ((PAIR, 128, QUAD1), (PAIR, 64, OCT1), outer),
        "p2": ((QUAD0, 128, QUAD0), (OCT0, 64, OCT0), partner),
        "o3": ((OCT0, 64, OCT2), (QUAD0, 64, OCT2), outer),
        "p3": ((QUAD1, 128, QUAD1), (OCT1, 64, OCT1), partner),
        "o4": ((OCT1, 64, OCT3), (QUAD1, 64, OCT3), outer),
    }
    arrivals = {
        "p1": ((PAIR, 256), (PAIR, 256)),
        "o1": ((QUAD0, 128), (OCT0, 64)),
        "o2": ((QUAD1, 128), (OCT1, 64)),
        "p2": ((OCT0, 64), (QUAD0, 128)),
        "o3": ((OCT2, 64), (OCT2, 64)),
        "p3": ((OCT1, 64), (QUAD1, 128)),
        "o4": ((OCT3, 64), (OCT3, 64)),
    }
    order = {name: i for i, name in enumerate(steps)}

    class Gather:
        def __init__(self, buf, send, recv):
            self.buf, self.send_sem, self.recv_sem = buf, send, recv

        def each(self, name, act):
            in_case, edge_case, device = steps[name]
            if in_case == edge_case:
                act(in_case, device)
            else:
                pl.when(inner)(lambda: act(in_case, device))
                pl.when(edge)(lambda: act(edge_case, device))

        def copy(self, name, case, device):
            src, rows, dst = case
            i = order[name]
            return remote(
                self.buf.at[pl.ds(src, rows)], self.buf.at[pl.ds(dst, rows)],
                self.send_sem.at[i], self.recv_sem.at[i], device,
            )

        def send(self, name):
            self.each(name, lambda case, device: self.copy(name, case, device).start())

        def sent(self, name):
            self.each(name, lambda case, device: self.copy(name, case, device).wait_send())

        def arrive(self, name):
            i, device = order[name], steps[name][2]

            def act(case):
                spot = self.buf.at[pl.ds(case[0], case[1])]
                remote(spot, spot, self.send_sem.at[i], self.recv_sem.at[i], device).wait_recv()

            in_case, edge_case = arrivals[name]
            if in_case == edge_case:
                act(in_case)
            else:
                pl.when(inner)(lambda: act(in_case))
                pl.when(edge)(lambda: act(edge_case))

    kv_ring = Gather(kv, kv_send, kv_recv)
    qd_ring = Gather(qd, qd_send, qd_recv)

    loads[0].wait()
    loads[1].wait()
    keys = nn(tok[...], wqkv[1]).astype(BF16)
    loads[2].wait()
    values = nn(tok[...], wqkv[2]).astype(BF16)
    project(keys, values)
    permute(kv)

    pl.semaphore_wait(barrier, len(peers) + 3)
    kv_ring.send("p1")
    kv_ring.send("o1")

    loads[3].wait()
    queries = (nn(tok[...], wqkv[0]) * (1.0 / math.sqrt(HD))).astype(BF16)
    loads[4].wait()
    loads[5].wait()
    upstream = nt(cot[...], wo[...]).astype(BF16)
    project(queries, upstream)
    permute(qd)

    def block(h, first, width, depth, mask, fresh):
        k, v = slice(h * 256, h * 256 + 128), slice(h * 256 + 128, h * 256 + 256)
        q_rows, d_rows = qd[first : first + width, k], qd[first : first + width, v]
        s = nt(kv[0:depth, k], q_rows)
        if mask is not None:
            s = jnp.where(mask[...] > 0.0, s, NEG)
        top = jnp.max(s, axis=0, keepdims=True)
        e = jnp.exp(s - top)
        if mask is not None:
            e = e * mask[...]
        inv = 1.0 / jnp.sum(e, axis=0, keepdims=True)
        p = e * inv
        p_low = p.astype(BF16)
        attended = tn(p_low, kv[0:depth, v]).astype(BF16)
        att_p[first : first + width, h * 128 : (h + 1) * 128] = attended
        product = d_rows.astype(F32) * attended.astype(F32)
        delta = jnp.sum(product.T, axis=0, keepdims=True)
        stat[h : h + 1, first : first + width] = top
        stat[2 + h : 3 + h, first : first + width] = inv
        stat[4 + h : 5 + h, first : first + width] = delta
        slope = (p * (nt(kv[0:depth, v], d_rows) - delta)).astype(BF16)
        gcat[first : first + width, h * 384 : h * 384 + 128] = (
            tn(slope, kv[0:depth, k]) * (1.0 / math.sqrt(HD))
        ).astype(BF16)
        dk = nn(slope[0:ROWS], q_rows)
        dv = nn(p_low[0:ROWS], d_rows)
        if fresh:
            grads[h, :, 0:128] = dk
            grads[h, :, 128:256] = dv
        else:
            grads[h, :, 0:128] += dk
            grads[h, :, 128:256] += dv

    block(0, 256, 256, ROWS, None, True)
    kv_ring.arrive("o1")
    kv_ring.send("p2")
    block(1, 256, 256, ROWS, None, True)
    kv_ring.arrive("p1")
    kv_ring.send("o2")
    qd_ring.send("p1")
    qd_ring.send("o1")
    for h in range(HEADS):
        block(h, 128, 128, 768, mask_b, False)
    kv_ring.arrive("o2")
    kv_ring.send("p3")
    kv_ring.arrive("p2")
    kv_ring.send("o3")
    kv_ring.arrive("p3")
    kv_ring.send("o4")
    qd_ring.arrive("o1")
    qd_ring.send("p2")
    kv_ring.arrive("o3")
    kv_ring.arrive("o4")
    qd_ring.arrive("p1")
    qd_ring.send("o2")
    for h in range(HEADS):
        block(h, 0, 128, ALL, mask_a, False)

    st_copies = []
    for k in range(1, RING):
        spot = lax.rem(z + k, RING)
        slot = SLOTS[k - 1]
        power = 1
        digit = 0
        for d in range(RING):
            here = 1 - (spot - d) * (spot - d)
            here = (here + jnp.abs(here)) // 2
            digit = digit + here * (slot // 8**d % 8)
        copy = remote(
            stat.at[:, pl.ds(0, 256)], stat_g.at[digit], st_send.at[k - 1], st_recv.at[k - 1], peers[k - 1]
        )
        copy.start()
        st_copies.append(copy)

    qd_ring.arrive("o2")
    qd_ring.send("p3")
    qd_ring.arrive("p2")
    qd_ring.send("o3")

    class Scatter:
        def __init__(self, r):
            self.r = r
            self.copies = []

        def sems(self, i):
            return rs_send.at[self.r, i], rs_recv.at[self.r, i]

        def send(self, i, src, dst, device):
            copy = remote(src, dst, *self.sems(i), device)
            copy.start()
            self.copies.append(copy)

        def arrive(self, i, dst, device):
            remote(dst, dst, *self.sems(i), device).wait_recv()

        def compute(self, product):
            r = self.r
            for dx in (2, 1, 3, 0):
                target = lax.rem(x + dx, 4) * 2
                sib_out[r, dx] = product(target + 1 - core).astype(BF16)
                self.send(dx, sib_out.at[r, dx], sib_in.at[r, dx], sibling)
                own[r, dx] = product(target + core)

        def pair_sum(self, dx):
            r = self.r
            self.arrive(dx, sib_in.at[r, dx], sibling)
            return own[r, dx] + sib_in[r, dx].astype(F32)

        def first(self):
            r = self.r
            far[r] = self.pair_sum(2).astype(BF16)
            self.send(4, far.at[r, pl.ds(0, 256)], half_in.at[r, 0], right)
            self.send(5, far.at[r, pl.ds(256, 256)], half_in.at[r, 1], left)
            own[r, 1] = self.pair_sum(1)
            near[r, 0, 256:512] = own[r, 1, 256:512].astype(BF16)
            self.send(6, near.at[r, 0, pl.ds(256, 256)], near_in.at[r, 0, pl.ds(256, 256)], right)
            own[r, 3] = self.pair_sum(3)
            near[r, 1, 0:256] = own[r, 3, 0:256].astype(BF16)
            self.send(7, near.at[r, 1, pl.ds(0, 256)], near_in.at[r, 1, pl.ds(0, 256)], left)
            own[r, 0] = self.pair_sum(0)

        def second(self):
            r = self.r
            self.arrive(4, half_in.at[r, 0], right)
            near[r, 0, 0:256] = (own[r, 1, 0:256] + half_in[r, 0].astype(F32)).astype(BF16)
            self.send(8, near.at[r, 0, pl.ds(0, 256)], near_in.at[r, 0, pl.ds(0, 256)], right)
            self.arrive(5, half_in.at[r, 1], left)
            near[r, 1, 256:512] = (own[r, 3, 256:512] + half_in[r, 1].astype(F32)).astype(BF16)
            self.send(9, near.at[r, 1, pl.ds(256, 256)], near_in.at[r, 1, pl.ds(256, 256)], left)

        def last(self, into):
            r = self.r
            self.arrive(6, near_in.at[r, 0, pl.ds(256, 256)], right)
            self.arrive(7, near_in.at[r, 1, pl.ds(0, 256)], left)
            self.arrive(8, near_in.at[r, 0, pl.ds(0, 256)], right)
            self.arrive(9, near_in.at[r, 1, pl.ds(256, 256)], left)
            into[...] = (own[r, 0] + near_in[r, 0].astype(F32) + near_in[r, 1].astype(F32)).astype(BF16)

        def drain(self):
            for copy in self.copies:
                copy.wait_send()

    for h in range(HEADS):
        att[:, h * 128 : (h + 1) * 128] = nn(unperm[h], att_p[:, h * 128 : (h + 1) * 128]).astype(BF16)
    scatter_out = Scatter(0)
    scatter_out.compute(
        lambda target: nn(att[...], wo[:, pl.ds(pl.multiple_of(target * COLS, COLS), COLS)])
    )
    qd_ring.arrive("p3")
    qd_ring.send("o4")
    scatter_out.first()

    for k in range(1, RING):
        remote(
            stat_g.at[0], stat_g.at[0], st_send.at[k - 1], st_recv.at[k - 1], peers[k - 1]
        ).wait_recv()

    def far_block(h, first, depth, stats, mask):
        k, v = slice(h * 256, h * 256 + 128), slice(h * 256 + 128, h * 256 + 256)
        q_rows, d_rows = qd[first : first + 256, k], qd[first : first + 256, v]
        top, inv, delta = (stats[i : i + 1] for i in (h, 2 + h, 4 + h))
        p = jnp.exp(nt(kv[0:depth, k], q_rows) - top) * inv
        if mask is not None:
            p = p * mask[...]
        p_low = p.astype(BF16)
        slope = (p * (nt(kv[0:depth, v], d_rows) - delta)).astype(BF16)
        grads[h, 0:depth, 0:128] += nn(slope, q_rows)
        grads[h, 0:depth, 128:256] += nn(p_low, d_rows)

    for h in range(HEADS):
        far_block(h, PAIR, 256, stat_g[0], mask_p)
    quad_stat = jnp.concatenate([stat_g[1, :, 0:128], stat_g[2, :, 0:128]], 1)
    for h in range(HEADS):
        far_block(h, QUAD0, 128, quad_stat, mask_q)
    scatter_out.second()
    qd_ring.arrive("o3")
    qd_ring.arrive("o4")
    low_lanes = lax.broadcasted_iota(jnp.int32, (8, 128), 1) < 64
    oct_stat = jnp.concatenate(
        [
            jnp.where(low_lanes, stat_g[a, :, 0:128], pltpu.roll(stat_g[a + 1, :, 0:128], 64, 1))
            for a in (3, 5)
        ],
        1,
    )
    for h in range(HEADS):
        far_block(h, OCT0, 64, oct_stat, None)

    for h in range(HEADS):
        gcat[:, h * 384 + 128 : h * 384 + 384] = grads[h].astype(BF16)
        turned = nn(unperm[h], gcat[:, h * 384 : (h + 1) * 384]).astype(BF16)
        for part in range(3):
            gall[part, :, h * 128 : (h + 1) * 128] = turned[:, part * 128 : (part + 1) * 128]

    def back(target):
        rows = pl.ds(pl.multiple_of(target * COLS, COLS), COLS)
        return nt(gall[0], wqkv[0, rows]) + nt(gall[1], wqkv[1, rows]) + nt(gall[2], wqkv[2, rows])

    scatter_in = Scatter(1)
    scatter_in.compute(back)
    scatter_in.first()
    scatter_out.last(out_ref)
    scatter_in.second()
    scatter_in.last(ing_ref)

    for name in steps:
        kv_ring.sent(name)
        qd_ring.sent(name)
    for copy in st_copies:
        copy.wait_send()
    scatter_out.drain()
    scatter_in.drain()


def on_device(tokens, w_qkv, w_out, offsets, cotangent):
    whole = pl.BlockSpec(memory_space=pl.ANY)
    vmem = pl.BlockSpec(memory_space=pltpu.VMEM)
    return pl.pallas_call(
        kernel,
        out_shape=(jax.ShapeDtypeStruct((ROWS, COLS), BF16),) * 2,
        in_specs=[whole, whole, whole, pl.BlockSpec(memory_space=pltpu.SMEM), whole],
        out_specs=(vmem, vmem),
        scratch_shapes=[
            pltpu.VMEM((ROWS, MODEL), BF16),
            pltpu.VMEM((3, MODEL, COLS), BF16),
            pltpu.VMEM((COLS, MODEL), BF16),
            pltpu.VMEM((ROWS, MODEL), BF16),
            pltpu.VMEM((ROWS, 512), BF16),
            pltpu.VMEM((ALL, 512), BF16),
            pltpu.VMEM((ALL, 512), BF16),
            pltpu.VMEM((HEADS, ROWS, ROWS), BF16),
            pltpu.VMEM((HEADS, ROWS, ROWS), BF16),
            pltpu.VMEM((ALL, 128), F32),
            pltpu.VMEM((768, 128), F32),
            pltpu.VMEM((256, 256), F32),
            pltpu.VMEM((128, 256), F32),
            pltpu.VMEM((HEADS, ROWS, 256), F32),
            pltpu.VMEM((ROWS, 256), BF16),
            pltpu.VMEM((ROWS, 768), BF16),
            pltpu.VMEM((ROWS, 256), BF16),
            pltpu.VMEM((3, ROWS, 256), BF16),
            pltpu.VMEM((8, ROWS), F32),
            pltpu.VMEM((7, 8, 256), F32),
            pltpu.VMEM((2, 4, ROWS, COLS), F32),
            pltpu.VMEM((2, 4, ROWS, COLS), BF16),
            pltpu.VMEM((2, 4, ROWS, COLS), BF16),
            pltpu.VMEM((2, ROWS, COLS), BF16),
            pltpu.VMEM((2, 2, 256, COLS), BF16),
            pltpu.VMEM((2, 2, ROWS, COLS), BF16),
            pltpu.VMEM((2, 2, ROWS, COLS), BF16),
            pltpu.SemaphoreType.DMA((6,)),
            pltpu.SemaphoreType.DMA((7,)),
            pltpu.SemaphoreType.DMA((7,)),
            pltpu.SemaphoreType.DMA((7,)),
            pltpu.SemaphoreType.DMA((7,)),
            pltpu.SemaphoreType.DMA((7,)),
            pltpu.SemaphoreType.DMA((7,)),
            pltpu.SemaphoreType.DMA((2, 10)),
            pltpu.SemaphoreType.DMA((2, 10)),
        ],
        compiler_params=pltpu.CompilerParams(
            collective_id=0, has_side_effects=True, vmem_limit_bytes=52 * 1024 * 1024
        ),
    )(tokens, w_qkv, w_out, offsets, cotangent)


def solution(mesh):
    in_specs = (P("seq", None), P(None, None, "head"), P("head", None), P("head"), P("seq", None))
    out_specs = (P("seq", "head"), P("seq", "head"))
    return jax.shard_map(on_device, mesh=mesh, in_specs=in_specs, out_specs=out_specs, check_vma=False)
```

time: 214 us -> 63.5 us (0.30); the launches traced: 212 us -> 63.2 us
  matrix products: 77.5 us -> 0 us
  waiting for transfers between devices: 59.9 us -> 0 us
  Pallas kernels: 0 us -> 59.3 us
  starting transfers between devices: 31.9 us -> 0 us
  other arithmetic: 18.7 us -> 0 us
  between operations: 19.3 us -> 0.65 us
    dot_general x122 -> x0, matrix products: 77.5 us -> none  [the longest x30 16.1 us: spread_wide(): lax.dot_general(chooser.astype(jnp.float32), values, (((0,), (0,)), ((),...]
    pallas_call x0 -> x1, Pallas kernels: none -> 59.3 us  [on_device(): pl.pallas_call(kernel, out_shape=(jax.ShapeDtypeStruct((ROWS, COLS), BF16...]
    reduce_scatter x2 -> x0, waiting for transfers between devices: 39.2 us -> none  [the longest x1 39.2 us: on_device(): lax.psum_scatter(partial_in.astype(jnp.bfloat16), 'head', scatter_dimensi...]
    ppermute x12 -> x0, starting transfers between devices: 31.9 us -> none  [partner(): return lax.ppermute(value, axis, pairs)]
    ppermute x12 -> x0, waiting for transfers between devices: 20.7 us -> none  [partner(): return lax.ppermute(value, axis, pairs)]
    reduce_or x6 -> x0, other arithmetic: 5.17 us -> none  [spread_stat(): covered = jnp.any(chooser, axis=0)]
    select_n x6 -> x0, other arithmetic: 5.04 us -> none  [joined_rows(): jnp.where(upper_side, jnp.concatenate([far_part, own_part], 0), jnp.conca...]
    add x14 -> x0, other arithmetic: 2.52 us -> none  [the longest x6 2.47 us: shrink(): keeping + partner(sending.astype(jnp.bfloat16), 'seq', bit_pos).astype(se...]
  transfers between devices with their start and end apart: 14 -> 0, of which waited for: 7 -> 0; matrix products, arithmetic and copies ran while one was open for 26% -> 0% of each run, Pallas kernels for 0% -> 0%
where the time goes in v1:
time: 63.5 us; the launch traced here: 63.2 us
  Pallas kernels  59.3 us (93%)
  local copies, waits for them, and re-layouts  3.28 us (5%)
  between operations  0.65 us (1%)
    pallas_call x1, Pallas kernels, on_device(): pl.pallas_call(kernel, out_shape=(jax.ShapeDtypeStruct((ROWS, COLS), BF16...  59.3 us
    unnamed x6, local copies, waits for them, and re-layouts  3.28 us

profile of v1, /device:TPU:1, one launch (start us, length us, event | category | flops | bytes accessed | tf_op | source)
XLA Modules:
  0.0 63.2 jit_solution(8672576092511149363)
XLA Ops:
  0.6 0.0 copy-start
  0.6 1.2 %copy-done = bf16[256,2048]{1,0:T(8,128)(2,1)S(1)} copy-done((bf16[256,2048]{1,0:T(8,128)(2,1)S(1)}, bf16[256,2048]{1,0:T(8,128)(2,1)}, u32[]{:S(2)}) %copy-start) | copy-done | bytes 1048600
  1.9 0.0 copy-start.1
  1.9 0.7 %copy-done.1 = s32[2]{0:T(128)S(1)} copy-done((s32[2]{0:T(128)S(1)}, s32[2]{0:T(128)}, u32[]{:S(2)}) %copy-start.1) | copy-done | bytes 32
  2.5 59.3 %shard_map.68 = (bf16[512,256]{1,0:T(8,128)(2,1)S(1)}, bf16[512,256]{1,0:T(8,128)(2,1)S(1)}) custom-call(bf16[512,2048]{1,0:T(8,128)(2,1)} %tok_hbm.1, bf16[3,2048,256]{2,1,0:T(8,128)(2,1)} %wqkv_hbm.1, bf16[256,2048]{1,0:T(8,128)(2,1)S(1)} %copy-done, s32[2]{0:T(128)S(1)} %copy-done.1, bf16[512,2048]{1,0:T(8,128)(2,1)} %cot_hbm.1), custom_call_target="tpu_custom_call" | custom-call | tf_op jit(solution)/shard_map/pallas_call | solution.py:445
  61.8 0.7 %copy.9 = bf16[512,256]{1,0:T(8,128)(2,1)} copy(bf16[512,256]{1,0:T(8,128)(2,1)S(1)} %get-tuple-element.4) | data formatting | bytes 524288
  62.5 0.7 %copy.10 = bf16[512,256]{1,0:T(8,128)(2,1)} copy(bf16[512,256]{1,0:T(8,128)(2,1)S(1)} %get-tuple-element.5) | data formatting | bytes 524288
Async XLA Ops:
  0.6 1.2 %copy-start = (bf16[256,2048]{1,0:T(8,128)(2,1)S(1)}, bf16[256,2048]{1,0:T(8,128)(2,1)}, u32[]{:S(2)}) copy-start(bf16[256,2048]{1,0:T(8,128)(2,1)} %wo_hbm.1) | copy-start | bytes 3145732
  1.9 0.7 %copy-start.1 = (s32[2]{0:T(128)S(1)}, s32[2]{0:T(128)}, u32[]{:S(2)}) copy-start(s32[2]{0:T(128)} %off_ref.1) | copy-start | bytes 28

commit v2 on v1

v2 whole, which is shorter than its diff:
```python
import math

import jax
import jax.numpy as jnp
from jax import lax
from jax.experimental import pallas as pl
from jax.experimental.pallas import tpu as pltpu
from jax.sharding import PartitionSpec as P

MESH = pl.DeviceIdType.MESH
F32, BF16 = jnp.float32, jnp.bfloat16
ROWS = 512
MODEL = 2048
HD = 128
HEADS = 2
RING = 8
ALL = 1280
PAIR, QUAD0, QUAD1, OCT0, OCT1, OCT2, OCT3 = 512, 768, 896, 1024, 1088, 1152, 1216
COLS = 256
NEG = float("-inf")


def nn(a, b):
    return jnp.dot(a, b, preferred_element_type=F32)


def nt(a, b):
    return lax.dot_general(a, b, (((1,), (1,)), ((), ())), preferred_element_type=F32)


def tn(a, b):
    return lax.dot_general(a, b, (((0,), (0,)), ((), ())), preferred_element_type=F32)


def slot_table():
    tables = []
    for k in range(1, RING):
        code = 0
        for d in range(RING):
            source = (d - k) % RING
            inner = d % 4 in (1, 2)
            side = 1 if d % 2 == 1 else -1
            out_dist = (source - d) * side % RING
            in_dist = (d - source) * side % RING
            if source // 2 == d // 2:
                slot = 0
            elif source // 4 == d // 4:
                slot = 1 if source % 4 in (1, 2) else 2
            elif inner:
                slot = {2: 3, 3: 4}[in_dist] if in_dist in (2, 3) else {3: 5, 4: 6}[out_dist]
            else:
                slot = 2 + out_dist
            code += slot * 8**d
        tables.append(code)
    return tables


SLOTS = slot_table()


def kernel(
    tok_hbm, wqkv_hbm, wo_hbm, off_hbm, cot_hbm, out_ref, ing_ref,
    tok, wkv, wq, wo, cot, off_ref, raw, kv, qd, perm, unperm, mask_a, mask_b, mask_p, mask_q,
    grads, att_p, dq_p, gkv_p, att, gq, gkv, acc, stat, stat_g,
    own, sib_out, sib_in, far, half_in, near, near_in,
    load_sem, ring_send, ring_recv, st_send, st_recv, rs_send, rs_recv,
):
    seq = lax.axis_index("seq")
    head = lax.axis_index("head")
    z = lax.rem(seq, RING)
    base = seq - z
    odd = lax.rem(z, 2)
    partner = (base + z + 1 - 2 * odd, head)
    outer = (base + lax.rem(z + 2 * odd + RING - 1, RING), head)
    inner = lax.rem((lax.rem(z, 4) + 1) // 2, 2) == 1
    edge = jnp.logical_not(inner)
    x, core = head // 2, lax.rem(head, 2)
    sibling = (seq, head + 1 - 2 * core)
    right = (seq, lax.rem(x + 1, 4) * 2 + core)
    left = (seq, lax.rem(x + 3, 4) * 2 + core)

    loads = [
        pltpu.make_async_copy(off_hbm, off_ref, load_sem.at[0]),
        pltpu.make_async_copy(tok_hbm, tok, load_sem.at[1]),
    ]
    for h in range(HEADS):
        for part in range(2):
            loads.append(
                pltpu.make_async_copy(
                    wqkv_hbm.at[1 + part, :, pl.ds(h * 128, 128)],
                    wkv.at[:, pl.ds(h * 256 + part * 128, 128)],
                    load_sem.at[2 + 2 * h + part],
                )
            )
    late_loads = [
        pltpu.make_async_copy(wqkv_hbm.at[0], wq, load_sem.at[6]),
        pltpu.make_async_copy(cot_hbm, cot, load_sem.at[7]),
        pltpu.make_async_copy(wo_hbm, wo, load_sem.at[8]),
    ]
    for copy in loads:
        copy.start()

    barrier = pltpu.get_barrier_semaphore()
    peers = [(base + lax.rem(z + k, RING), head) for k in range(1, RING)]
    for device in peers + [sibling, right, left]:
        pl.semaphore_signal(barrier, inc=1, device_id=device, device_id_type=MESH)

    index = lax.broadcasted_iota(jnp.int32, (ROWS, 128), 0)
    lane = lax.broadcasted_iota(jnp.int32, (ROWS, 128), 1)

    def levels(key, query, start):
        far_end = jnp.maximum(key, query)
        count = jnp.full(key.shape, float(start), F32)
        for limit in (256, 128, 64):
            count = count + jnp.where(far_end < limit, 1.0, 0.0)
        return count

    mask_a[0:512] = levels(index, lane, 1)
    mask_a[512:768] = levels(index[0:256], lane[0:256], 0)
    quad_mask = levels(index[0:128], lane[0:128], -1)
    mask_a[768:896] = quad_mask
    mask_a[896:1024] = quad_mask
    mask_a[1024:1280] = jnp.where(lane[0:256] < 64, 1.0, 0.0)
    mask_b[0:512] = levels(index, lane + 128, 1)
    mask_b[512:768] = levels(index[0:256], lane[0:256] + 128, 0)
    mask_p[:, 0:128] = levels(index[0:256], lane[0:256], 0)
    mask_p[:, 128:256] = levels(index[0:256], lane[0:256] + 128, 0)
    mask_q[:, 0:128] = quad_mask
    mask_q[:, 128:256] = quad_mask
    for copy in late_loads:
        copy.start()

    loads[0].wait()
    for h in range(HEADS):
        offset = off_ref[h]
        block = index >> 6
        turned = ((block & 1) << 2) | (block & 2) | (block >> 2)
        old = ((index & 63) << 3) + ((turned + offset) & 7)
        rest = ((index & 7) - offset) & 7
        new = ((((rest & 1) << 2) | (rest & 2) | (rest >> 2)) << 6) + (index >> 3)
        for c in range(ROWS // 128):
            perm[h, :, c * 128 : (c + 1) * 128] = jnp.where(old == lane + c * 128, 1.0, 0.0).astype(BF16)
            unperm[h, :, c * 128 : (c + 1) * 128] = jnp.where(new == lane + c * 128, 1.0, 0.0).astype(BF16)

    def remote(src, dst, send, recv, device):
        return pltpu.make_async_remote_copy(
            src_ref=src, dst_ref=dst, send_sem=send, recv_sem=recv, device_id=device, device_id_type=MESH
        )

    steps = {
        "p1": ((0, 128, PAIR), (0, 128, PAIR), partner),
        "p1b": ((128, 128, PAIR + 128), (128, 128, PAIR + 128), partner),
        "o1": ((0, 128, QUAD0), (0, 64, OCT0), outer),
        "o2": ((PAIR, 128, QUAD1), (PAIR, 64, OCT1), outer),
        "p2": ((QUAD0, 128, QUAD0), (OCT0, 64, OCT0), partner),
        "o3": ((OCT0, 64, OCT2), (QUAD0, 64, OCT2), outer),
        "p3": ((QUAD1, 128, QUAD1), (OCT1, 64, OCT1), partner),
        "o4": ((OCT1, 64, OCT3), (QUAD1, 64, OCT3), outer),
    }
    arrivals = {
        "p1": ((PAIR, 128), (PAIR, 128)),
        "p1b": ((PAIR + 128, 128), (PAIR + 128, 128)),
        "o1": ((QUAD0, 128), (OCT0, 64)),
        "o2": ((QUAD1, 128), (OCT1, 64)),
        "p2": ((OCT0, 64), (QUAD0, 128)),
        "o3": ((OCT2, 64), (OCT2, 64)),
        "p3": ((OCT1, 64), (QUAD1, 128)),
        "o4": ((OCT3, 64), (OCT3, 64)),
    }
    order = {name: i for i, name in enumerate(steps)}
    onward = {"o1": "p2", "p1": "o2", "o2": "p3", "p2": "o3", "p3": "o4"}

    class Gather:
        def __init__(self, buf, send, recv):
            self.buf, self.send_sem, self.recv_sem = buf, send, recv

        def each(self, name, act):
            in_case, edge_case, device = steps[name]
            if in_case == edge_case:
                act(in_case, device)
            else:
                pl.when(inner)(lambda: act(in_case, device))
                pl.when(edge)(lambda: act(edge_case, device))

        def copy(self, name, case, device):
            src, rows, dst = case
            i = order[name]
            return remote(
                self.buf.at[pl.ds(src, rows)], self.buf.at[pl.ds(dst, rows)],
                self.send_sem.at[i], self.recv_sem.at[i], device,
            )

        def send(self, name):
            self.each(name, lambda case, device: self.copy(name, case, device).start())

        def sent(self, name):
            self.each(name, lambda case, device: self.copy(name, case, device).wait_send())

        def arrive(self, name):
            i, device = order[name], steps[name][2]

            def act(case):
                spot = self.buf.at[pl.ds(case[0], case[1])]
                remote(spot, spot, self.send_sem.at[i], self.recv_sem.at[i], device).wait_recv()

            in_case, edge_case = arrivals[name]
            if in_case == edge_case:
                act(in_case)
            else:
                pl.when(inner)(lambda: act(in_case))
                pl.when(edge)(lambda: act(edge_case))

        def own(self):
            self.send("o1")
            self.send("p1")

        def on(self, name):
            self.arrive(name)
            self.send(onward[name])

    rings = [Gather(buf.at[h], ring_send.at[i, h], ring_recv.at[i, h]) for i, buf in enumerate((kv, qd)) for h in range(HEADS)]
    kv0, kv1, qd0, qd1 = rings

    for copy in loads[1:]:
        copy.wait()
    raw[...] = nn(tok[...], wkv[...]).astype(BF16)
    kv[0, 0:ROWS] = nn(perm[0], raw[:, 0:256]).astype(BF16)
    pl.semaphore_wait(barrier, len(peers) + 3)
    kv0.own()
    kv[1, 0:ROWS] = nn(perm[1], raw[:, 256:512]).astype(BF16)
    late_loads[0].wait()
    queries = (nn(tok[...], wq[...]) * (1.0 / math.sqrt(HD))).astype(BF16)
    kv1.own()
    late_loads[1].wait()
    late_loads[2].wait()
    upstream = nt(cot[...], wo[...]).astype(BF16)
    for h in range(HEADS):
        raw[:, h * 256 : h * 256 + 128] = queries[:, h * 128 : (h + 1) * 128]
        raw[:, h * 256 + 128 : h * 256 + 256] = upstream[:, h * 128 : (h + 1) * 128]
    kv0.on("o1")
    kv0.on("p1")
    kv0.send("p1b")
    for h in range(HEADS):
        qd[h, 0:ROWS] = nn(perm[h], raw[:, h * 256 : (h + 1) * 256]).astype(BF16)

    first, second = slice(0, 128), slice(128, 256)

    def block(h, start, width, depth, mask, fresh):
        q_rows, d_rows = qd[h, start : start + width, first], qd[h, start : start + width, second]
        s = nt(kv[h, 0:depth, first], q_rows)
        if mask is not None:
            s = jnp.where(mask[...] > 0.0, s, NEG)
        top = jnp.max(s, axis=0, keepdims=True)
        e = jnp.exp(s - top)
        if mask is not None:
            e = e * mask[...]
        inv = 1.0 / jnp.sum(e, axis=0, keepdims=True)
        p = e * inv
        p_low = p.astype(BF16)
        attended = tn(p_low, kv[h, 0:depth, second]).astype(BF16)
        att_p[h, start : start + width] = attended
        product = d_rows.astype(F32) * attended.astype(F32)
        delta = jnp.sum(product.T, axis=0, keepdims=True)
        stat[h : h + 1, start : start + width] = top
        stat[2 + h : 3 + h, start : start + width] = inv
        stat[4 + h : 5 + h, start : start + width] = delta
        slope = (p * (nt(kv[h, 0:depth, second], d_rows) - delta)).astype(BF16)
        dq_p[h, start : start + width] = (tn(slope, kv[h, 0:depth, first]) * (1.0 / math.sqrt(HD))).astype(BF16)
        dk = nn(slope[0:ROWS], q_rows)
        dv = nn(p_low[0:ROWS], d_rows)
        if fresh:
            grads[h, :, first] = dk
            grads[h, :, second] = dv
        else:
            grads[h, :, first] += dk
            grads[h, :, second] += dv

    block(0, 256, 256, ROWS, None, True)
    kv1.on("o1")
    kv1.on("p1")
    block(1, 256, 256, ROWS, None, True)
    kv0.on("o2")
    kv0.on("p2")
    kv0.arrive("p1b")
    block(0, 128, 128, 768, mask_b, False)
    kv1.on("o2")
    kv1.send("p1b")
    kv1.on("p2")
    qd0.own()
    qd1.own()
    kv0.on("p3")
    kv1.on("p3")
    qd0.on("o1")

    def inner_passes():
        qd0.on("p1")
        qd1.on("o1")

    pl.when(inner)(inner_passes)
    kv1.arrive("p1b")
    block(1, 128, 128, 768, mask_b, False)

    def edge_passes():
        qd1.on("o1")
        qd0.on("p1")

    pl.when(edge)(edge_passes)
    pl.when(inner)(lambda: qd1.on("p1"))
    kv0.arrive("o3")
    kv0.arrive("o4")
    block(0, 0, 128, ALL, mask_a, False)
    pl.when(edge)(lambda: qd1.on("p1"))
    kv1.arrive("o3")
    kv1.arrive("o4")
    block(1, 0, 128, ALL, mask_a, False)

    st_copies = []
    for k in range(1, RING):
        spot = lax.rem(z + k, RING)
        slot = SLOTS[k - 1]
        digit = 0
        for d in range(RING):
            here = 1 - (spot - d) * (spot - d)
            here = (here + jnp.abs(here)) // 2
            digit = digit + here * (slot // 8**d % 8)
        copy = remote(
            stat.at[:, pl.ds(0, 256)], stat_g.at[digit], st_send.at[k - 1], st_recv.at[k - 1], peers[k - 1]
        )
        copy.start()
        st_copies.append(copy)

    qd0.on("o2")
    qd0.on("p2")

    class Scatter:
        def __init__(self, r):
            self.r = r
            self.copies = []

        def sems(self, i):
            return rs_send.at[self.r, i], rs_recv.at[self.r, i]

        def send(self, i, src, dst, device):
            copy = remote(src, dst, *self.sems(i), device)
            copy.start()
            self.copies.append(copy)

        def arrive(self, i, dst, device):
            remote(dst, dst, *self.sems(i), device).wait_recv()

        def part(self, dx, product):
            r = self.r
            both = product(dx)
            low, high = both[:, 0:COLS], both[:, COLS : 2 * COLS]
            sib_out[r, dx] = jnp.where(core == 0, high, low).astype(BF16)
            self.send(dx, sib_out.at[r, dx], sib_in.at[r, dx], sibling)
            own[r, dx] = jnp.where(core == 0, low, high)

        def pair_sum(self, dx):
            r = self.r
            self.arrive(dx, sib_in.at[r, dx], sibling)
            return own[r, dx] + sib_in[r, dx].astype(F32)

        def halves(self):
            r = self.r
            far[r] = self.pair_sum(2).astype(BF16)
            self.send(4, far.at[r, pl.ds(0, 256)], half_in.at[r, 0], right)
            self.send(5, far.at[r, pl.ds(256, 256)], half_in.at[r, 1], left)

        def direct(self):
            r = self.r
            own[r, 1] = self.pair_sum(1)
            near[r, 0, 256:512] = own[r, 1, 256:512].astype(BF16)
            self.send(6, near.at[r, 0, pl.ds(256, 256)], near_in.at[r, 0, pl.ds(256, 256)], right)
            own[r, 3] = self.pair_sum(3)
            near[r, 1, 0:256] = own[r, 3, 0:256].astype(BF16)
            self.send(7, near.at[r, 1, pl.ds(0, 256)], near_in.at[r, 1, pl.ds(0, 256)], left)
            own[r, 0] = self.pair_sum(0)

        def summed(self):
            r = self.r
            self.arrive(4, half_in.at[r, 0], right)
            near[r, 0, 0:256] = (own[r, 1, 0:256] + half_in[r, 0].astype(F32)).astype(BF16)
            self.send(8, near.at[r, 0, pl.ds(0, 256)], near_in.at[r, 0, pl.ds(0, 256)], right)
            self.arrive(5, half_in.at[r, 1], left)
            near[r, 1, 256:512] = (own[r, 3, 256:512] + half_in[r, 1].astype(F32)).astype(BF16)
            self.send(9, near.at[r, 1, pl.ds(256, 256)], near_in.at[r, 1, pl.ds(256, 256)], left)

        def last(self, into):
            r = self.r
            self.arrive(6, near_in.at[r, 0, pl.ds(256, 256)], right)
            self.arrive(7, near_in.at[r, 1, pl.ds(0, 256)], left)
            self.arrive(8, near_in.at[r, 0, pl.ds(0, 256)], right)
            self.arrive(9, near_in.at[r, 1, pl.ds(256, 256)], left)
            into[...] = (own[r, 0] + near_in[r, 0].astype(F32) + near_in[r, 1].astype(F32)).astype(BF16)

        def drain(self):
            for copy in self.copies:
                copy.wait_send()

    def chip_span(dx):
        return pl.ds(pl.multiple_of(lax.rem(x + dx, 4) * 2 * COLS, 2 * COLS), 2 * COLS)

    for h in range(HEADS):
        att[:, h * 128 : (h + 1) * 128] = nn(unperm[h], att_p[h]).astype(BF16)
    scatter_out = Scatter(0)

    def forward_part(dx):
        scatter_out.part(dx, lambda dx: nn(att[...], wo[:, chip_span(dx)]))

    forward_part(2)
    qd1.on("o2")
    qd1.on("p2")
    qd0.send("p1b")
    qd1.send("p1b")
    forward_part(1)
    forward_part(3)
    scatter_out.halves()
    qd0.on("p3")
    forward_part(0)
    scatter_out.direct()
    for h in range(HEADS):
        gq[:, h * 128 : (h + 1) * 128] = nn(unperm[h], dq_p[h]).astype(BF16)
    qd1.on("p3")
    for dx in (2, 1, 3, 0):
        acc[dx] = nt(gq[...], wq[chip_span(dx)])
    for k in range(1, RING):
        remote(
            stat_g.at[0], stat_g.at[0], st_send.at[k - 1], st_recv.at[k - 1], peers[k - 1]
        ).wait_recv()
    quad_stat = jnp.concatenate([stat_g[1, :, 0:128], stat_g[2, :, 0:128]], 1)
    low_lanes = lax.broadcasted_iota(jnp.int32, (8, 128), 1) < 64
    oct_stat = jnp.concatenate(
        [
            jnp.where(low_lanes, stat_g[a, :, 0:128], pltpu.roll(stat_g[a + 1, :, 0:128], 64, 1))
            for a in (3, 5)
        ],
        1,
    )

    def far_block(h, start, depth, stats, mask):
        q_rows, d_rows = qd[h, start : start + 256, first], qd[h, start : start + 256, second]
        top, inv, delta = (stats[i : i + 1] for i in (h, 2 + h, 4 + h))
        p = jnp.exp(nt(kv[h, 0:depth, first], q_rows) - top) * inv
        if mask is not None:
            p = p * mask[...]
        p_low = p.astype(BF16)
        slope = (p * (nt(kv[h, 0:depth, second], d_rows) - delta)).astype(BF16)
        grads[h, 0:depth, first] += nn(slope, q_rows)
        grads[h, 0:depth, second] += nn(p_low, d_rows)

    def to_tokens(h):
        gkv_p[h] = grads[h].astype(BF16)
        gkv[:, h * 256 : (h + 1) * 256] = nn(unperm[h], gkv_p[h]).astype(BF16)

    far_block(0, QUAD0, 128, quad_stat, mask_q)
    far_block(1, QUAD0, 128, quad_stat, mask_q)
    qd0.arrive("p1b")
    far_block(0, PAIR, 256, stat_g[0], mask_p)
    scatter_out.summed()
    qd0.arrive("o3")
    qd0.arrive("o4")
    far_block(0, OCT0, 64, oct_stat, None)
    to_tokens(0)
    qd1.arrive("p1b")
    far_block(1, PAIR, 256, stat_g[0], mask_p)
    qd1.arrive("o3")
    qd1.arrive("o4")
    far_block(1, OCT0, 64, oct_stat, None)
    to_tokens(1)

    scatter_in = Scatter(1)

    def back(dx):
        return acc[dx] + nt(gkv[...], wkv[chip_span(dx)])

    for dx in (2, 1, 3):
        scatter_in.part(dx, back)
    scatter_in.halves()
    scatter_in.part(0, back)
    scatter_in.direct()
    scatter_out.last(out_ref)
    scatter_in.summed()
    scatter_in.last(ing_ref)

    for name in steps:
        for ring in rings:
            ring.sent(name)
    for copy in st_copies:
        copy.wait_send()
    scatter_out.drain()
    scatter_in.drain()


def on_device(tokens, w_qkv, w_out, offsets, cotangent):
    whole = pl.BlockSpec(memory_space=pl.ANY)
    vmem = pl.BlockSpec(memory_space=pltpu.VMEM)
    return pl.pallas_call(
        kernel,
        out_shape=(jax.ShapeDtypeStruct((ROWS, COLS), BF16),) * 2,
        in_specs=[whole] * 5,
        out_specs=(vmem, vmem),
        scratch_shapes=[
            pltpu.VMEM((ROWS, MODEL), BF16),
            pltpu.VMEM((MODEL, 512), BF16),
            pltpu.VMEM((MODEL, 256), BF16),
            pltpu.VMEM((256, MODEL), BF16),
            pltpu.VMEM((ROWS, MODEL), BF16),
            pltpu.SMEM((HEADS,), jnp.int32),
            pltpu.VMEM((ROWS, 512), BF16),
            pltpu.VMEM((HEADS, ALL, 256), BF16),
            pltpu.VMEM((HEADS, ALL, 256), BF16),
            pltpu.VMEM((HEADS, ROWS, ROWS), BF16),
            pltpu.VMEM((HEADS, ROWS, ROWS), BF16),
            pltpu.VMEM((ALL, 128), F32),
            pltpu.VMEM((768, 128), F32),
            pltpu.VMEM((256, 256), F32),
            pltpu.VMEM((128, 256), F32),
            pltpu.VMEM((HEADS, ROWS, 256), F32),
            pltpu.VMEM((HEADS, ROWS, 128), BF16),
            pltpu.VMEM((HEADS, ROWS, 128), BF16),
            pltpu.VMEM((HEADS, ROWS, 256), BF16),
            pltpu.VMEM((ROWS, 256), BF16),
            pltpu.VMEM((ROWS, 256), BF16),
            pltpu.VMEM((ROWS, 512), BF16),
            pltpu.VMEM((4, ROWS, 2 * COLS), F32),
            pltpu.VMEM((8, ROWS), F32),
            pltpu.VMEM((7, 8, 256), F32),
            pltpu.VMEM((2, 4, ROWS, COLS), F32),
            pltpu.VMEM((2, 4, ROWS, COLS), BF16),
            pltpu.VMEM((2, 4, ROWS, COLS), BF16),
            pltpu.VMEM((2, ROWS, COLS), BF16),
            pltpu.VMEM((2, 2, 256, COLS), BF16),
            pltpu.VMEM((2, 2, ROWS, COLS), BF16),
            pltpu.VMEM((2, 2, ROWS, COLS), BF16),
            pltpu.SemaphoreType.DMA((9,)),
            pltpu.SemaphoreType.DMA((2, HEADS, 8)),
            pltpu.SemaphoreType.DMA((2, HEADS, 8)),
            pltpu.SemaphoreType.DMA((7,)),
            pltpu.SemaphoreType.DMA((7,)),
            pltpu.SemaphoreType.DMA((2, 10)),
            pltpu.SemaphoreType.DMA((2, 10)),
        ],
        compiler_params=pltpu.CompilerParams(
            collective_id=0, has_side_effects=True, vmem_limit_bytes=52 * 1024 * 1024 + 512 * 1024
        ),
    )(tokens, w_qkv, w_out, offsets, cotangent)


def solution(mesh):
    in_specs = (P("seq", None), P(None, None, "head"), P("head", None), P("head"), P("seq", None))
    out_specs = (P("seq", "head"), P("seq", "head"))
    return jax.shard_map(on_device, mesh=mesh, in_specs=in_specs, out_specs=out_specs, check_vma=False)
```

time: 63.5 us -> 55.7 us (0.88)
  Pallas kernels: 59.3 us -> 52.9 us
  local copies, waits for them, and re-layouts: 3.28 us -> 2.06 us
    pallas_call x1, Pallas kernels: 59.3 us -> 52.9 us  [on_device(): pl.pallas_call(kernel, out_shape=(jax.ShapeDtypeStruct((ROWS, COLS), BF16...]
    unnamed x6 -> x4, local copies, waits for them, and re-layouts: 3.28 us -> 2.06 us
where the time goes in v2:
time: 55.7 us; the launch traced here: 55.6 us
  Pallas kernels  52.9 us (95%)
  local copies, waits for them, and re-layouts  2.06 us (4%)
  between operations  0.65 us (1%)
    pallas_call x1, Pallas kernels, on_device(): pl.pallas_call(kernel, out_shape=(jax.ShapeDtypeStruct((ROWS, COLS), BF16...  52.9 us
    unnamed x4, local copies, waits for them, and re-layouts  2.06 us

profile of v2, /device:TPU:1, one launch (start us, length us, event | category | flops | bytes accessed | tf_op | source)
XLA Modules:
  0.0 55.6 jit_solution(11917136659099060452)
XLA Ops:
  0.6 0.0 copy-start
  0.6 0.6 %copy-done = s32[2]{0:T(128)S(1)} copy-done((s32[2]{0:T(128)S(1)}, s32[2]{0:T(128)}, u32[]{:S(2)}) %copy-start) | copy-done | bytes 32
  1.3 52.9 %shard_map.68 = (bf16[512,256]{1,0:T(8,128)(2,1)S(1)}, bf16[512,256]{1,0:T(8,128)(2,1)S(1)}) custom-call(bf16[512,2048]{1,0:T(8,128)(2,1)} %tok_hbm.1, bf16[3,2048,256]{2,1,0:T(8,128)(2,1)} %wqkv_hbm.1, bf16[256,2048]{1,0:T(8,128)(2,1)} %wo_hbm.1, s32[2]{0:T(128)S(1)} %copy-done, bf16[512,2048]{1,0:T(8,128)(2,1)} %cot_hbm.1), custom_call_target="tpu_custom_call" | custom-call | tf_op jit(solution)/shard_map/pallas_call | solution.py:498
  54.2 0.7 %copy.9 = bf16[512,256]{1,0:T(8,128)(2,1)} copy(bf16[512,256]{1,0:T(8,128)(2,1)S(1)} %get-tuple-element.4) | data formatting | bytes 524288
  54.9 0.7 %copy.10 = bf16[512,256]{1,0:T(8,128)(2,1)} copy(bf16[512,256]{1,0:T(8,128)(2,1)S(1)} %get-tuple-element.5) | data formatting | bytes 524288
Async XLA Ops:
  0.6 0.7 %copy-start = (s32[2]{0:T(128)S(1)}, s32[2]{0:T(128)}, u32[]{:S(2)}) copy-start(s32[2]{0:T(128)} %off_hbm.1) | copy-start | bytes 28

commit v3 on v2

--- a/solution.py
+++ b/solution.py
@@ -59,11 +59,11 @@
 
 
 def kernel(
-    tok_hbm, wqkv_hbm, wo_hbm, off_hbm, cot_hbm, out_ref, ing_ref,
+    tok_hbm, wqkv_hbm, wo_hbm, off_hbm, cot_hbm, both_ref,
     tok, wkv, wq, wo, cot, off_ref, raw, kv, qd, perm, unperm, mask_a, mask_b, mask_p, mask_q,
-    grads, att_p, dq_p, gkv_p, att, gq, gkv, acc, stat, stat_g,
+    grads, keep_a, keep_b, keep_c, att_p, dq_p, gkv_p, att, gq, gkv, acc, stat, stat_g,
     own, sib_out, sib_in, far, half_in, near, near_in,
-    load_sem, ring_send, ring_recv, st_send, st_recv, rs_send, rs_recv,
+    load_sem, ring_send, ring_recv, st_send, st_recv, rs_send, rs_recv, turn_sem,
 ):
     seq = lax.axis_index("seq")
     head = lax.axis_index("head")
@@ -226,26 +226,31 @@
     raw[...] = nn(tok[...], wkv[...]).astype(BF16)
     kv[0, 0:ROWS] = nn(perm[0], raw[:, 0:256]).astype(BF16)
     pl.semaphore_wait(barrier, len(peers) + 3)
+    pl.when(core == 1)(lambda: pl.semaphore_wait(turn_sem, 1))
     kv0.own()
+    pl.when(core == 0)(lambda: pl.semaphore_signal(turn_sem, inc=1, device_id=sibling, device_id_type=MESH))
     kv[1, 0:ROWS] = nn(perm[1], raw[:, 256:512]).astype(BF16)
+    kv1.own()
     late_loads[0].wait()
     queries = (nn(tok[...], wq[...]) * (1.0 / math.sqrt(HD))).astype(BF16)
-    kv1.own()
     late_loads[1].wait()
     late_loads[2].wait()
     upstream = nt(cot[...], wo[...]).astype(BF16)
     for h in range(HEADS):
         raw[:, h * 256 : h * 256 + 128] = queries[:, h * 128 : (h + 1) * 128]
         raw[:, h * 256 + 128 : h * 256 + 256] = upstream[:, h * 128 : (h + 1) * 128]
+    kv0.on("p1")
     kv0.on("o1")
-    kv0.on("p1")
-    kv0.send("p1b")
+    pl.when(edge)(lambda: kv0.send("p1b"))
     for h in range(HEADS):
         qd[h, 0:ROWS] = nn(perm[h], raw[:, h * 256 : (h + 1) * 256]).astype(BF16)
+    kv1.on("p1")
+    kv1.on("o1")
+    pl.when(edge)(lambda: kv1.send("p1b"))
 
     first, second = slice(0, 128), slice(128, 256)
 
-    def block(h, start, width, depth, mask, fresh):
+    def forward(h, start, width, depth, mask, keep):
         q_rows, d_rows = qd[h, start : start + width, first], qd[h, start : start + width, second]
         s = nt(kv[h, 0:depth, first], q_rows)
         if mask is not None:
@@ -256,18 +261,23 @@
             e = e * mask[...]
         inv = 1.0 / jnp.sum(e, axis=0, keepdims=True)
         p = e * inv
-        p_low = p.astype(BF16)
-        attended = tn(p_low, kv[h, 0:depth, second]).astype(BF16)
+        if keep is not None:
+            keep[...] = p
+        attended = tn(p.astype(BF16), kv[h, 0:depth, second]).astype(BF16)
         att_p[h, start : start + width] = attended
         product = d_rows.astype(F32) * attended.astype(F32)
         delta = jnp.sum(product.T, axis=0, keepdims=True)
         stat[h : h + 1, start : start + width] = top
         stat[2 + h : 3 + h, start : start + width] = inv
         stat[4 + h : 5 + h, start : start + width] = delta
+        return p, delta
+
+    def backward(h, start, width, depth, p, delta, fresh):
+        q_rows, d_rows = qd[h, start : start + width, first], qd[h, start : start + width, second]
         slope = (p * (nt(kv[h, 0:depth, second], d_rows) - delta)).astype(BF16)
         dq_p[h, start : start + width] = (tn(slope, kv[h, 0:depth, first]) * (1.0 / math.sqrt(HD))).astype(BF16)
         dk = nn(slope[0:ROWS], q_rows)
-        dv = nn(p_low[0:ROWS], d_rows)
+        dv = nn(p[0:ROWS].astype(BF16), d_rows)
         if fresh:
             grads[h, :, first] = dk
             grads[h, :, second] = dv
@@ -275,44 +285,59 @@
             grads[h, :, first] += dk
             grads[h, :, second] += dv
 
-    block(0, 256, 256, ROWS, None, True)
-    kv1.on("o1")
-    kv1.on("p1")
-    block(1, 256, 256, ROWS, None, True)
+    def block(h, start, width, depth, mask, fresh):
+        p, delta = forward(h, start, width, depth, mask, None)
+        backward(h, start, width, depth, p, delta, fresh)
+
+    forward(0, 256, 256, ROWS, None, keep_c.at[0])
     kv0.on("o2")
+    forward(1, 256, 256, ROWS, None, keep_c.at[1])
+    kv1.on("o2")
     kv0.on("p2")
+    kv1.on("p2")
+
+    def pair_rest(low, high):
+        low.send("p1b")
+        high.send("p1b")
+
+    def query_own():
+        qd0.own()
+        qd1.own()
+
+    def edge_own():
+        query_own()
+        pair_rest(qd0, qd1)
+
+    pl.when(inner)(lambda: pair_rest(kv0, kv1))
+    pl.when(edge)(edge_own)
+    backward(0, 256, 256, ROWS, keep_c[0], stat[4:5, 256:512], True)
+    kv0.on("p3")
+    backward(1, 256, 256, ROWS, keep_c[1], stat[5:6, 256:512], True)
+    kv1.on("p3")
+    pl.when(inner)(query_own)
     kv0.arrive("p1b")
     block(0, 128, 128, 768, mask_b, False)
-    kv1.on("o2")
-    kv1.send("p1b")
-    kv1.on("p2")
-    qd0.own()
-    qd1.own()
-    kv0.on("p3")
-    kv1.on("p3")
-    qd0.on("o1")
-
-    def inner_passes():
-        qd0.on("p1")
-        qd1.on("o1")
-
-    pl.when(inner)(inner_passes)
-    kv1.arrive("p1b")
-    block(1, 128, 128, 768, mask_b, False)
-
-    def edge_passes():
-        qd1.on("o1")
-        qd0.on("p1")
-
-    pl.when(edge)(edge_passes)
-    pl.when(inner)(lambda: qd1.on("p1"))
     kv0.arrive("o3")
     kv0.arrive("o4")
-    block(0, 0, 128, ALL, mask_a, False)
-    pl.when(edge)(lambda: qd1.on("p1"))
+
+    def inner_passes(ring):
+        ring.on("o1")
+        ring.on("p1")
+
+    forward(0, 0, 128, ALL, mask_a, keep_a.at[0])
+    pl.when(inner)(lambda: inner_passes(qd0))
+    kv1.arrive("p1b")
+    forward(1, 128, 128, 768, mask_b, keep_b)
     kv1.arrive("o3")
     kv1.arrive("o4")
-    block(1, 0, 128, ALL, mask_a, False)
+    pl.when(inner)(lambda: inner_passes(qd1))
+
+    def edge_passes():
+        qd0.on("p1")
+        qd0.on("o1")
+
+    pl.when(edge)(edge_passes)
+    forward(1, 0, 128, ALL, mask_a, keep_a.at[1])
 
     st_copies = []
     for k in range(1, RING):
@@ -329,8 +354,8 @@
         copy.start()
         st_copies.append(copy)
 
-    qd0.on("o2")
-    qd0.on("p2")
+    pl.when(inner)(lambda: qd0.on("o2"))
+    pl.when(edge)(lambda: qd1.on("o1"))
 
     class Scatter:
         def __init__(self, r):
@@ -375,7 +400,6 @@
             own[r, 3] = self.pair_sum(3)
             near[r, 1, 0:256] = own[r, 3, 0:256].astype(BF16)
             self.send(7, near.at[r, 1, pl.ds(0, 256)], near_in.at[r, 1, pl.ds(0, 256)], left)
-            own[r, 0] = self.pair_sum(0)
 
         def summed(self):
             r = self.r
@@ -388,11 +412,12 @@
 
         def last(self, into):
             r = self.r
+            mine = self.pair_sum(0)
             self.arrive(6, near_in.at[r, 0, pl.ds(256, 256)], right)
             self.arrive(7, near_in.at[r, 1, pl.ds(0, 256)], left)
             self.arrive(8, near_in.at[r, 0, pl.ds(0, 256)], right)
             self.arrive(9, near_in.at[r, 1, pl.ds(256, 256)], left)
-            into[...] = (own[r, 0] + near_in[r, 0].astype(F32) + near_in[r, 1].astype(F32)).astype(BF16)
+            into[...] = (mine + near_in[r, 0].astype(F32) + near_in[r, 1].astype(F32)).astype(BF16)
 
         def drain(self):
             for copy in self.copies:
@@ -409,21 +434,26 @@
         scatter_out.part(dx, lambda dx: nn(att[...], wo[:, chip_span(dx)]))
 
     forward_part(2)
-    qd1.on("o2")
+    pl.when(edge)(lambda: qd1.on("p1"))
+    forward_part(1)
+
+    def inner_more():
+        qd1.on("o2")
+        pair_rest(qd0, qd1)
+
+    pl.when(inner)(inner_more)
+    scatter_out.halves()
+    forward_part(3)
+    forward_part(0)
+    qd0.on("p2")
+    backward(1, 128, 128, 768, keep_b[...], stat[5:6, 128:256], False)
+    pl.when(edge)(lambda: qd0.on("o2"))
+    backward(0, 0, 128, ALL, keep_a[0], stat[4:5, 0:128], False)
     qd1.on("p2")
-    qd0.send("p1b")
-    qd1.send("p1b")
-    forward_part(1)
-    forward_part(3)
-    scatter_out.halves()
+    pl.when(edge)(lambda: qd1.on("o2"))
+    backward(1, 0, 128, ALL, keep_a[1], stat[5:6, 0:128], False)
+    scatter_out.direct()
     qd0.on("p3")
-    forward_part(0)
-    scatter_out.direct()
-    for h in range(HEADS):
-        gq[:, h * 128 : (h + 1) * 128] = nn(unperm[h], dq_p[h]).astype(BF16)
-    qd1.on("p3")
-    for dx in (2, 1, 3, 0):
-        acc[dx] = nt(gq[...], wq[chip_span(dx)])
     for k in range(1, RING):
         remote(
             stat_g.at[0], stat_g.at[0], st_send.at[k - 1], st_recv.at[k - 1], peers[k - 1]
@@ -454,6 +484,11 @@
         gkv[:, h * 256 : (h + 1) * 256] = nn(unperm[h], gkv_p[h]).astype(BF16)
 
     far_block(0, QUAD0, 128, quad_stat, mask_q)
+    for h in range(HEADS):
+        gq[:, h * 128 : (h + 1) * 128] = nn(unperm[h], dq_p[h]).astype(BF16)
+    qd1.on("p3")
+    for dx in (2, 1, 3, 0):
+        acc[dx] = nt(gq[...], wq[chip_span(dx)])
     far_block(1, QUAD0, 128, quad_stat, mask_q)
     qd0.arrive("p1b")
     far_block(0, PAIR, 256, stat_g[0], mask_p)
@@ -474,14 +509,15 @@
     def back(dx):
         return acc[dx] + nt(gkv[...], wkv[chip_span(dx)])
 
-    for dx in (2, 1, 3):
+    for dx in (2, 1):
         scatter_in.part(dx, back)
     scatter_in.halves()
+    scatter_in.part(3, back)
+    scatter_in.direct()
     scatter_in.part(0, back)
-    scatter_in.direct()
-    scatter_out.last(out_ref)
+    scatter_out.last(both_ref.at[0])
     scatter_in.summed()
-    scatter_in.last(ing_ref)
+    scatter_in.last(both_ref.at[1])
 
     for name in steps:
         for ring in rings:
@@ -495,11 +531,11 @@
 def on_device(tokens, w_qkv, w_out, offsets, cotangent):
     whole = pl.BlockSpec(memory_space=pl.ANY)
     vmem = pl.BlockSpec(memory_space=pltpu.VMEM)
-    return pl.pallas_call(
+    both = pl.pallas_call(
         kernel,
-        out_shape=(jax.ShapeDtypeStruct((ROWS, COLS), BF16),) * 2,
+        out_shape=jax.ShapeDtypeStruct((2, ROWS, COLS), BF16),
         in_specs=[whole] * 5,
-        out_specs=(vmem, vmem),
+        out_specs=vmem,
         scratch_shapes=[
             pltpu.VMEM((ROWS, MODEL), BF16),
             pltpu.VMEM((MODEL, 512), BF16),
@@ -516,6 +552,9 @@
             pltpu.VMEM((768, 128), F32),
             pltpu.VMEM((256, 256), F32),
             pltpu.VMEM((128, 256), F32),
+            pltpu.VMEM((HEADS, ROWS, 256), F32),
+            pltpu.VMEM((HEADS, ALL, 128), F32),
+            pltpu.VMEM((768, 128), F32),
             pltpu.VMEM((HEADS, ROWS, 256), F32),
             pltpu.VMEM((HEADS, ROWS, 128), BF16),
             pltpu.VMEM((HEADS, ROWS, 128), BF16),
@@ -540,11 +579,13 @@
             pltpu.SemaphoreType.DMA((7,)),
             pltpu.SemaphoreType.DMA((2, 10)),
             pltpu.SemaphoreType.DMA((2, 10)),
+            pltpu.SemaphoreType.REGULAR,
         ],
         compiler_params=pltpu.CompilerParams(
             collective_id=0, has_side_effects=True, vmem_limit_bytes=52 * 1024 * 1024 + 512 * 1024
         ),
     )(tokens, w_qkv, w_out, offsets, cotangent)
+    return (both[0], both[1])
 
 
 def solution(mesh):

time: 55.7 us -> 55.5 us (level)
  local copies, waits for them, and re-layouts: 2.06 us -> 1.47 us
    unnamed x4 -> x2, local copies, waits for them, and re-layouts: 2.06 us -> 0.65 us
    squeeze x0 -> x1, local copies, waits for them, and re-layouts: none -> 0.82 us  [on_device(): return (both[0], both[1])]
where the time goes in v3:
time: 55.5 us; the launch traced here: 55.4 us
  Pallas kernels  53.3 us (96%)
  local copies, waits for them, and re-layouts  1.47 us (3%)
  between operations  0.65 us (1%)
    pallas_call x1, Pallas kernels, on_device(): pl.pallas_call(kernel, out_shape=jax.ShapeDtypeStruct((2, ROWS, COLS), BF...  53.3 us

profile of v3, /device:TPU:1, one launch (start us, length us, event | category | flops | bytes accessed | tf_op | source)
XLA Modules:
  0.0 55.4 jit_solution(7515862139261436811)
XLA Ops:
  0.6 0.0 copy-start
  0.6 0.6 %copy-done = s32[2]{0:T(128)S(1)} copy-done((s32[2]{0:T(128)S(1)}, s32[2]{0:T(128)}, u32[]{:S(2)}) %copy-start) | copy-done | bytes 32
  1.3 53.3 %shard_map.68 = bf16[2,512,256]{2,1,0:T(8,128)(2,1)S(1)} custom-call(bf16[512,2048]{1,0:T(8,128)(2,1)} %tok_hbm.1, bf16[3,2048,256]{2,1,0:T(8,128)(2,1)} %wqkv_hbm.1, bf16[256,2048]{1,0:T(8,128)(2,1)} %wo_hbm.1, s32[2]{0:T(128)S(1)} %copy-done, bf16[512,2048]{1,0:T(8,128)(2,1)} %cot_hbm.1), custom_call_target="tpu_custom_call" | custom-call | tf_op jit(solution)/shard_map/pallas_call | solution.py:534
  54.6 0.8 %slice_bitcast_fusion = (bf16[512,256]{1,0:T(8,128)(2,1)}, bf16[512,256]{1,0:T(8,128)(2,1)}) fusion(bf16[2,512,256]{2,1,0:T(8,128)(2,1)S(1)} %shard_map.68), kind=kLoop, calls=%fused_computation | loop fusion | bytes 1048576 | tf_op jit(solution)/shard_map/squeeze | solution.py:588
Async XLA Ops:
  0.6 0.7 %copy-start = (s32[2]{0:T(128)S(1)}, s32[2]{0:T(128)}, u32[]{:S(2)}) copy-start(s32[2]{0:T(128)} %off_hbm.1) | copy-start | bytes 28

commit v4 on v2

--- a/solution.py
+++ b/solution.py
@@ -59,7 +59,7 @@
 
 
 def kernel(
-    tok_hbm, wqkv_hbm, wo_hbm, off_hbm, cot_hbm, out_ref, ing_ref,
+    tok_hbm, wqkv_hbm, wo_hbm, off_hbm, cot_hbm, both_ref,
     tok, wkv, wq, wo, cot, off_ref, raw, kv, qd, perm, unperm, mask_a, mask_b, mask_p, mask_q,
     grads, att_p, dq_p, gkv_p, att, gq, gkv, acc, stat, stat_g,
     own, sib_out, sib_in, far, half_in, near, near_in,
@@ -375,7 +375,6 @@
             own[r, 3] = self.pair_sum(3)
             near[r, 1, 0:256] = own[r, 3, 0:256].astype(BF16)
             self.send(7, near.at[r, 1, pl.ds(0, 256)], near_in.at[r, 1, pl.ds(0, 256)], left)
-            own[r, 0] = self.pair_sum(0)
 
         def summed(self):
             r = self.r
@@ -388,11 +387,12 @@
 
         def last(self, into):
             r = self.r
+            mine = self.pair_sum(0)
             self.arrive(6, near_in.at[r, 0, pl.ds(256, 256)], right)
             self.arrive(7, near_in.at[r, 1, pl.ds(0, 256)], left)
             self.arrive(8, near_in.at[r, 0, pl.ds(0, 256)], right)
             self.arrive(9, near_in.at[r, 1, pl.ds(256, 256)], left)
-            into[...] = (own[r, 0] + near_in[r, 0].astype(F32) + near_in[r, 1].astype(F32)).astype(BF16)
+            into[...] = (mine + near_in[r, 0].astype(F32) + near_in[r, 1].astype(F32)).astype(BF16)
 
         def drain(self):
             for copy in self.copies:
@@ -479,9 +479,9 @@
     scatter_in.halves()
     scatter_in.part(0, back)
     scatter_in.direct()
-    scatter_out.last(out_ref)
+    scatter_out.last(both_ref.at[0])
     scatter_in.summed()
-    scatter_in.last(ing_ref)
+    scatter_in.last(both_ref.at[1])
 
     for name in steps:
         for ring in rings:
@@ -495,11 +495,11 @@
 def on_device(tokens, w_qkv, w_out, offsets, cotangent):
     whole = pl.BlockSpec(memory_space=pl.ANY)
     vmem = pl.BlockSpec(memory_space=pltpu.VMEM)
-    return pl.pallas_call(
+    both = pl.pallas_call(
         kernel,
-        out_shape=(jax.ShapeDtypeStruct((ROWS, COLS), BF16),) * 2,
+        out_shape=jax.ShapeDtypeStruct((2, ROWS, COLS), BF16),
         in_specs=[whole] * 5,
-        out_specs=(vmem, vmem),
+        out_specs=vmem,
         scratch_shapes=[
             pltpu.VMEM((ROWS, MODEL), BF16),
             pltpu.VMEM((MODEL, 512), BF16),
@@ -545,6 +545,7 @@
             collective_id=0, has_side_effects=True, vmem_limit_bytes=52 * 1024 * 1024 + 512 * 1024
         ),
     )(tokens, w_qkv, w_out, offsets, cotangent)
+    return (both[0], both[1])
 
 
 def solution(mesh):

time: 55.7 us -> 55.4 us (level)
  local copies, waits for them, and re-layouts: 2.06 us -> 1.47 us
    unnamed x4 -> x2, local copies, waits for them, and re-layouts: 2.06 us -> 0.65 us
    squeeze x0 -> x1, local copies, waits for them, and re-layouts: none -> 0.82 us  [on_device(): return (both[0], both[1])]
where the time goes in v4:
time: 55.4 us; the launch traced here: 55.3 us
  Pallas kernels  53.2 us (96%)
  local copies, waits for them, and re-layouts  1.47 us (3%)
  between operations  0.65 us (1%)
    pallas_call x1, Pallas kernels, on_device(): pl.pallas_call(kernel, out_shape=jax.ShapeDtypeStruct((2, ROWS, COLS), BF...  53.2 us

profile of v4, /device:TPU:1, one launch (start us, length us, event | category | flops | bytes accessed | tf_op | source)
XLA Modules:
  0.0 55.3 jit_solution(4467262066311459267)
XLA Ops:
  0.6 0.0 copy-start
  0.6 0.6 %copy-done = s32[2]{0:T(128)S(1)} copy-done((s32[2]{0:T(128)S(1)}, s32[2]{0:T(128)}, u32[]{:S(2)}) %copy-start) | copy-done | bytes 32
  1.3 53.2 %shard_map.68 = bf16[2,512,256]{2,1,0:T(8,128)(2,1)S(1)} custom-call(bf16[512,2048]{1,0:T(8,128)(2,1)} %tok_hbm.1, bf16[3,2048,256]{2,1,0:T(8,128)(2,1)} %wqkv_hbm.1, bf16[256,2048]{1,0:T(8,128)(2,1)} %wo_hbm.1, s32[2]{0:T(128)S(1)} %copy-done, bf16[512,2048]{1,0:T(8,128)(2,1)} %cot_hbm.1), custom_call_target="tpu_custom_call" | custom-call | tf_op jit(solution)/shard_map/pallas_call | solution.py:498
  54.5 0.8 %slice_bitcast_fusion = (bf16[512,256]{1,0:T(8,128)(2,1)}, bf16[512,256]{1,0:T(8,128)(2,1)}) fusion(bf16[2,512,256]{2,1,0:T(8,128)(2,1)S(1)} %shard_map.68), kind=kLoop, calls=%fused_computation | loop fusion | bytes 1048576 | tf_op jit(solution)/shard_map/squeeze | solution.py:548
Async XLA Ops:
  0.6 0.7 %copy-start = (s32[2]{0:T(128)S(1)}, s32[2]{0:T(128)}, u32[]{:S(2)}) copy-start(s32[2]{0:T(128)} %off_hbm.1) | copy-start | bytes 28

commit v5 on v3

--- a/solution.py
+++ b/solution.py
@@ -368,7 +368,7 @@
         def send(self, i, src, dst, device):
             copy = remote(src, dst, *self.sems(i), device)
             copy.start()
-            self.copies.append(copy)
+            self.copies.append((src, dst, i, device))
 
         def arrive(self, i, dst, device):
             remote(dst, dst, *self.sems(i), device).wait_recv()
@@ -389,8 +389,8 @@
         def halves(self):
             r = self.r
             far[r] = self.pair_sum(2).astype(BF16)
-            self.send(4, far.at[r, pl.ds(0, 256)], half_in.at[r, 0], right)
-            self.send(5, far.at[r, pl.ds(256, 256)], half_in.at[r, 1], left)
+            for i, device in ((0, right), (1, left)):
+                remote(far.at[r, pl.ds(i * 256, 256)], half_in.at[r, i], *self.sems(4 + i), device).start()
 
         def direct(self):
             r = self.r
@@ -420,8 +420,12 @@
             into[...] = (mine + near_in[r, 0].astype(F32) + near_in[r, 1].astype(F32)).astype(BF16)
 
         def drain(self):
-            for copy in self.copies:
-                copy.wait_send()
+            for src, dst, i, device in self.copies:
+                remote(src, dst, *self.sems(i), device).wait_send()
+            for i, device in ((0, right), (1, left)):
+                remote(
+                    far.at[self.r, pl.ds(i * 256, 256)], half_in.at[self.r, i], *self.sems(4 + i), device
+                ).wait_send()
 
     def chip_span(dx):
         return pl.ds(pl.multiple_of(lax.rem(x + dx, 4) * 2 * COLS, 2 * COLS), 2 * COLS)
@@ -434,6 +438,7 @@
         scatter_out.part(dx, lambda dx: nn(att[...], wo[:, chip_span(dx)]))
 
     forward_part(2)
+    pl.when(core == 0)(scatter_out.halves)
     pl.when(edge)(lambda: qd1.on("p1"))
     forward_part(1)
 
@@ -442,9 +447,9 @@
         pair_rest(qd0, qd1)
 
     pl.when(inner)(inner_more)
-    scatter_out.halves()
     forward_part(3)
     forward_part(0)
+    pl.when(core == 1)(scatter_out.halves)
     qd0.on("p2")
     backward(1, 128, 128, 768, keep_b[...], stat[5:6, 128:256], False)
     pl.when(edge)(lambda: qd0.on("o2"))
@@ -509,10 +514,11 @@
     def back(dx):
         return acc[dx] + nt(gkv[...], wkv[chip_span(dx)])
 
-    for dx in (2, 1):
-        scatter_in.part(dx, back)
-    scatter_in.halves()
+    scatter_in.part(2, back)
+    pl.when(core == 0)(scatter_in.halves)
+    scatter_in.part(1, back)
     scatter_in.part(3, back)
+    pl.when(core == 1)(scatter_in.halves)
     scatter_in.direct()
     scatter_in.part(0, back)
     scatter_out.last(both_ref.at[0])

time: 55.5 us -> 55 us (level)
  Pallas kernels: 53.3 us -> 52.7 us
    pallas_call x1, Pallas kernels: 53.3 us -> 52.7 us  [on_device(): pl.pallas_call(kernel, out_shape=jax.ShapeDtypeStruct((2, ROWS, COLS), BF...]
where the time goes in v5:
time: 55 us; the launch traced here: 54.9 us
  Pallas kernels  52.7 us (96%)
  local copies, waits for them, and re-layouts  1.47 us (3%)
  between operations  0.65 us (1%)
    pallas_call x1, Pallas kernels, on_device(): pl.pallas_call(kernel, out_shape=jax.ShapeDtypeStruct((2, ROWS, COLS), BF...  52.7 us

profile of v5, /device:TPU:1, one launch (start us, length us, event | category | flops | bytes accessed | tf_op | source)
XLA Modules:
  0.0 54.9 jit_solution(17872164898811901040)
XLA Ops:
  0.6 0.0 copy-start
  0.6 0.6 %copy-done = s32[2]{0:T(128)S(1)} copy-done((s32[2]{0:T(128)S(1)}, s32[2]{0:T(128)}, u32[]{:S(2)}) %copy-start) | copy-done | bytes 32
  1.3 52.7 %shard_map.68 = bf16[2,512,256]{2,1,0:T(8,128)(2,1)S(1)} custom-call(bf16[512,2048]{1,0:T(8,128)(2,1)} %tok_hbm.1, bf16[3,2048,256]{2,1,0:T(8,128)(2,1)} %wqkv_hbm.1, bf16[256,2048]{1,0:T(8,128)(2,1)} %wo_hbm.1, s32[2]{0:T(128)S(1)} %copy-done, bf16[512,2048]{1,0:T(8,128)(2,1)} %cot_hbm.1), custom_call_target="tpu_custom_call" | custom-call | tf_op jit(solution)/shard_map/pallas_call | solution.py:540
  54.0 0.8 %slice_bitcast_fusion = (bf16[512,256]{1,0:T(8,128)(2,1)}, bf16[512,256]{1,0:T(8,128)(2,1)}) fusion(bf16[2,512,256]{2,1,0:T(8,128)(2,1)S(1)} %shard_map.68), kind=kLoop, calls=%fused_computation | loop fusion | bytes 1048576 | tf_op jit(solution)/shard_map/squeeze | solution.py:594
Async XLA Ops:
  0.6 0.7 %copy-start = (s32[2]{0:T(128)S(1)}, s32[2]{0:T(128)}, u32[]{:S(2)}) copy-start(s32[2]{0:T(128)} %off_hbm.1) | copy-start | bytes 28
